TPU v7x, 128 devices: a whole 4x4x4 slice. The times are simulated.
128 devices in a mesh: gx: 8 (over x, core), gy: 16 (over z, y).
Axes of the slice: x: 4, y: 4, z: 4, core: 2. Of those that a mesh axis runs over, the one named last changes fastest.
Arguments:
- image: float32 [128, 256, 256], P('gx', 'gy'), may hold values from -6 to 6
- conduct: float32 [128, 256, 256], P('gx', 'gy'), may hold values from 4 to 400
Outputs:
- blurred: float32 [128, 256, 256], P('gx', 'gy')
All inputs are finite; a program needn't handle non-finite values.
Results may differ from a plain program's by a relative error of at most 0.0003.
Values sent between devices are 32-bit elements; how exact they have to be, the bound alone decides.
A program may use at most 192 MiB of HBM per device.

v0:
```python
import jax
import jax.numpy as jnp
from jax import lax
from jax.sharding import PartitionSpec as P

COARSE_SWEEPS = 8


def extended(cells, sides, width):
    for axis, dim in sides:
        count = lax.axis_size(axis)
        ends = count - 1
        head = lax.slice_in_dim(cells, 0, width, axis=dim)
        tail = lax.slice_in_dim(cells, cells.shape[dim] - width, cells.shape[dim], axis=dim)
        cells = jnp.concatenate(
            [
                lax.ppermute(tail, axis, [(i, (i + 1) % count) for i in range(ends)]),
                cells,
                lax.ppermute(head, axis, [((i + 1) % count, i) for i in range(ends)]),
            ],
            axis=dim,
        )
    return cells


def coarsen(values):
    size_x, size_y, size_z = values.shape
    blocks = values.reshape(size_x // 2, 2, size_y // 2, 2, size_z // 2, 2)
    return blocks.sum(axis=(1, 3, 5)) * 0.125


def refine(values):
    return jnp.repeat(jnp.repeat(jnp.repeat(values, 2, 0), 2, 1), 2, 2)


def shift_up(values):
    return jnp.pad(values[:, :, 1:], ((0, 0), (0, 0), (0, 1)))


def shift_down(values):
    return jnp.pad(values[:, :, :-1], ((0, 0), (0, 0), (1, 0)))


def neighbour_sums(values, conductance, inside, weight_scale):
    cond_mid = conductance[1:-1, 1:-1]
    mid_inside = inside[1:-1, 1:-1]
    weighted = jnp.zeros(cond_mid.shape, jnp.float32)
    total_weight = jnp.zeros(cond_mid.shape, jnp.float32)
    windows = [
        (slice(2, None), slice(1, -1)),
        (slice(None, -2), slice(1, -1)),
        (slice(1, -1), slice(2, None)),
        (slice(1, -1), slice(None, -2)),
    ]
    for window in windows:
        coupling = mid_inside * inside[window] * (cond_mid + conductance[window]) * weight_scale
        weighted = weighted + coupling * values[window]
        total_weight = total_weight + coupling
    vals_mid = values[1:-1, 1:-1]
    for mover in (shift_up, shift_down):
        coupling = mid_inside * mover(mid_inside) * (cond_mid + mover(cond_mid)) * weight_scale
        weighted = weighted + coupling * mover(vals_mid)
        total_weight = total_weight + coupling
    return (weighted, total_weight)


def half_sweep(values, source, conductance, inside, row_ids, col_ids, parity, weight_scale):
    weighted, total_weight = neighbour_sums(values, conductance, inside, weight_scale)
    update = (source + weighted) / (1.0 + total_weight)
    depth_ids = jnp.arange(values.shape[2], dtype=jnp.int32)
    colour = (row_ids[:, None, None] + col_ids[None, :, None] + depth_ids[None, None, :]) % 2
    return jnp.where(colour == parity, update, values[1:-1, 1:-1])


def index_frame(offset, extent, rim_width, grid_extent):
    indices = offset + jnp.arange(-rim_width, extent + rim_width, dtype=jnp.int32)
    inside = jnp.logical_and(indices >= 0, indices < grid_extent).astype(jnp.float32)
    return (indices, inside)


def rim_one(values):
    return extended(values, (("gx", 0), ("gy", 1)), 1)


def prepare(conductance, weight_scale):
    size_x, size_y, size_z = conductance.shape
    rim_width = 1
    cond_pad = extended(conductance, (("gx", 0), ("gy", 1)), rim_width)
    row_ids, row_inside = index_frame(
        lax.axis_index("gx") * size_x, size_x, rim_width, size_x * lax.axis_size("gx")
    )
    col_ids, col_inside = index_frame(
        lax.axis_index("gy") * size_y, size_y, rim_width, size_y * lax.axis_size("gy")
    )
    inside = jnp.broadcast_to(
        row_inside[:, None, None] * col_inside[None, :, None],
        (size_x + 2 * rim_width, size_y + 2 * rim_width, size_z),
    )
    return (cond_pad, inside, row_ids, col_ids, rim_width, weight_scale)


def sweep(estimate, source, context):
    cond_pad, inside, row_ids, col_ids, rim_width, weight_scale = context
    red_done = half_sweep(
        rim_one(estimate), source, cond_pad, inside, row_ids[1:-1], col_ids[1:-1], 0, weight_scale
    )
    return half_sweep(
        rim_one(red_done), source, cond_pad, inside, row_ids[1:-1], col_ids[1:-1], 1, weight_scale
    )


def residual(estimate, source, context):
    cond_pad, inside, row_ids, col_ids, rim_width, weight_scale = context
    weighted, total_weight = neighbour_sums(rim_one(estimate), cond_pad, inside, weight_scale)
    return source - ((1.0 + total_weight) * estimate - weighted)


def shards(image, conduct):
    scales = [0.5 / 4.0**grid_level for grid_level in range(4)]
    conductances = [conduct]
    for grid_level in range(3):
        conductances.append(coarsen(conductances[-1]))
    spread_levels = 3
    estimate = image
    source = image
    saved = []
    for grid_level in range(spread_levels):
        context = prepare(conductances[grid_level], scales[grid_level])
        source_pad = source
        for repeat in range(2):
            estimate = sweep(estimate, source, context)
        saved.append((estimate, source, source_pad, context))
        source = coarsen(residual(estimate, source, context))
        estimate = jnp.zeros(source.shape, jnp.float32)
    context = prepare(conductances[3], scales[3])
    estimate = jnp.zeros(source.shape, jnp.float32)
    for repeat in range(COARSE_SWEEPS):
        estimate = sweep(estimate, source, context)
    up_levels = (2, 1, 0)
    for grid_level in up_levels:
        kept, source, source_pad, context = saved[grid_level]
        estimate = kept + refine(estimate)
        for repeat in range(2):
            estimate = sweep(estimate, source, context)
    return estimate


def solution(mesh):
    return jax.shard_map(
        shards,
        mesh=mesh,
        in_specs=(P("gx", "gy", None), P("gx", "gy", None)),
        out_specs=P("gx", "gy", None),
        check_vma=False,
    )
```

profile of v0, /device:TPU:100, one launch (start us, length us, event | category | flops | bytes accessed | tf_op | source)
XLA Modules:
  0.0 820.1 jit_solution(17696214033572149532)
XLA Ops:
  16.6 18.1 %reshape.376 = f32[8,2,8,2,128,2]{5,4,3,2,1,0:T(8,128)} reshape(f32[16,16,256]{2,1,0:T(8,128)S(1)} %copy-done) | data formatting | bytes 524288 | tf_op jit(solution)/shard_map/reshape | solution.py:28
  34.8 7.0 reduce_sum.55
  53.1 4.8 collective-permute-start.4
  59.9 6.0 collective-permute-start.5
  81.6 6.0 collective-permute-start.10
  89.6 5.7 collective-permute-done.11
  128.6 5.5 collective-permute-start.28
  143.7 6.0 collective-permute-start.22
  151.8 6.0 collective-permute-start.29
  160.3 18.1 %reshape.375 = f32[8,2,8,2,128,2]{5,4,3,2,1,0:T(8,128)} reshape(f32[16,16,256]{2,1,0:T(8,128)S(1)} %fusion.54) | data formatting | bytes 524288 | tf_op jit(solution)/shard_map/reshape | solution.py:28
  178.5 7.0 reduce_sum.54
  198.2 6.0 collective-permute-start.34
  206.3 5.6 collective-permute-done.35
  243.9 5.6 collective-permute-start.52
  258.5 6.0 collective-permute-start.46
  266.5 6.0 collective-permute-start.53
  296.4 6.0 collective-permute-start.58
  304.4 5.6 collective-permute-done.59
  333.4 4.4 collective-permute-start.66
  339.8 5.6 collective-permute-done.67
  374.9 3.9 collective-permute-start.83
  391.3 3.9 collective-permute-start.87
  522.9 3.9 collective-permute-start.119
  539.5 3.9 collective-permute-start.123
  (672 shorter events, 659.8 us)
Async XLA Ops:
  0.8 52.2 %collective-permute-start.2 = (f32[1,16,256]{2,1,0:T(8,128)S(1)}, f32[1,16,256]{2,1,0:T(8,128)S(1)}, u32[]{:S(2)}, u32[]{:S(2)}) collective-permute-start(f32[1,16,256]{2,1,0:T(8,128)S(1)} %get-tuple-element.83), channel_id=1, source_target_pairs={{0,16},{16,32},{32,48},{48,64},{64,80},{80,96},{96,112},{1,17},{17... | collective-permute-start | bytes 49160 | tf_op jit(solution)/shard_map/ppermute | solution.py:17
  2.7 50.3 %collective-permute-start = (f32[1,16,256]{2,1,0:T(8,128)S(1)}, f32[1,16,256]{2,1,0:T(8,128)S(1)}, u32[]{:S(2)}, u32[]{:S(2)}) collective-permute-start(f32[1,16,256]{2,1,0:T(8,128)S(1)} %get-tuple-element.84), channel_id=1, source_target_pairs={{16,0},{32,16},{48,32},{64,48},{80,64},{96,80},{112,96},{17,1},{33... | collective-permute-start | bytes 49160 | tf_op jit(solution)/shard_map/ppermute | solution.py:19
  7.1 52.7 %collective-permute-start.3 = (f32[1,16,256]{2,1,0:T(8,128)S(1)}, f32[1,16,256]{2,1,0:T(8,128)S(1)}, u32[]{:S(2)}, u32[]{:S(2)}) collective-permute-start(f32[1,16,256]{2,1,0:T(8,128)S(1)} %get-tuple-element.88), channel_id=1, source_target_pairs={{0,16},{16,32},{32,48},{48,64},{64,80},{80,96},{96,112},{1,17},{17... | collective-permute-start | bytes 49160 | tf_op jit(solution)/shard_map/ppermute | solution.py:17
  9.0 50.8 %collective-permute-start.1 = (f32[1,16,256]{2,1,0:T(8,128)S(1)}, f32[1,16,256]{2,1,0:T(8,128)S(1)}, u32[]{:S(2)}, u32[]{:S(2)}) collective-permute-start(f32[1,16,256]{2,1,0:T(8,128)S(1)} %get-tuple-element.87), channel_id=1, source_target_pairs={{16,0},{32,16},{48,32},{64,48},{80,64},{96,80},{112,96},{17,1},{33... | collective-permute-start | bytes 49160 | tf_op jit(solution)/shard_map/ppermute | solution.py:19
  13.3 123.4 %collective-permute-start.25 = (f32[1,8,128]{2,1,0:T(8,128)}, f32[1,8,128]{2,1,0:T(8,128)S(1)}, u32[]{:S(2)}, u32[]{:S(2)}) collective-permute-start(f32[1,8,128]{2,1,0:T(8,128)} %broadcast.751), channel_id=1, source_target_pairs={{16,0},{32,16},{48,32},{64,48},{80,64},{96,80},{112,96},{17,1},{33... | collective-permute-start | bytes 12296 | tf_op jit(solution)/shard_map/ppermute | solution.py:19
  53.1 14.9 %collective-permute-start.4 = (f32[18,1,256]{2,1,0:T(1,128)S(1)}, f32[18,1,256]{2,1,0:T(1,128)S(1)}, u32[]{:S(2)}, u32[]{:S(2)}) collective-permute-start(f32[18,1,256]{2,1,0:T(1,128)S(1)} %get-tuple-element.46), channel_id=1, source_target_pairs={{1,0},{2,1},{3,2},{4,3},{5,4},{6,5},{7,6},{8,7},{9,8},{10,9},{11,1... | collective-permute-start | bytes 55304 | tf_op jit(solution)/shard_map/ppermute | solution.py:19
  59.9 13.7 %collective-permute-start.5 = (f32[18,1,256]{2,1,0:T(1,128)S(1)}, f32[18,1,256]{2,1,0:T(1,128)S(1)}, u32[]{:S(2)}, u32[]{:S(2)}) collective-permute-start(f32[18,1,256]{2,1,0:T(1,128)S(1)} %get-tuple-element.47), channel_id=1, source_target_pairs={{1,0},{2,1},{3,2},{4,3},{5,4},{6,5},{7,6},{8,7},{9,8},{10,9},{11,1... | collective-permute-start | bytes 55304 | tf_op jit(solution)/shard_map/ppermute | solution.py:19
  68.0 70.6 %collective-permute-start.27 = (f32[1,8,128]{2,1,0:T(8,128)}, f32[1,8,128]{2,1,0:T(8,128)S(1)}, u32[]{:S(2)}, u32[]{:S(2)}) collective-permute-start(f32[1,8,128]{2,1,0:T(8,128)} %broadcast.751), channel_id=1, source_target_pairs={{0,16},{16,32},{32,48},{48,64},{64,80},{80,96},{96,112},{1,17},{17... | collective-permute-start | bytes 12296 | tf_op jit(solution)/shard_map/ppermute | solution.py:17
  69.9 45.0 %collective-permute-start.24 = (f32[1,8,128]{2,1,0:T(8,128)}, f32[1,8,128]{2,1,0:T(8,128)S(1)}, u32[]{:S(2)}, u32[]{:S(2)}) collective-permute-start(f32[1,8,128]{2,1,0:T(8,128)} %get-tuple-element.144), channel_id=1, source_target_pairs={{16,0},{32,16},{48,32},{64,48},{80,64},{96,80},{112,96},{17,1},{33... | collective-permute-start | bytes 12296 | tf_op jit(solution)/shard_map/ppermute | solution.py:19
  112.5 139.1 %collective-permute-start.49 = (f32[1,4,64]{2,1,0:T(4,128)S(1)}, f32[1,4,64]{2,1,0:T(4,128)S(1)}, u32[]{:S(2)}, u32[]{:S(2)}) collective-permute-start(f32[1,4,64]{2,1,0:T(4,128)S(1)} %broadcast.761), channel_id=1, source_target_pairs={{16,0},{32,16},{48,32},{64,48},{80,64},{96,80},{112,96},{17,1},{33... | collective-permute-start | bytes 3080 | tf_op jit(solution)/shard_map/ppermute | solution.py:19
  128.6 56.8 %collective-permute-start.28 = (f32[10,1,128]{2,1,0:T(1,128)S(1)}, f32[10,1,128]{2,1,0:T(1,128)S(1)}, u32[]{:S(2)}, u32[]{:S(2)}) collective-permute-start(f32[10,1,128]{2,1,0:T(1,128)S(1)} %get-tuple-element.106), channel_id=1, source_target_pairs={{1,0},{2,1},{3,2},{4,3},{5,4},{6,5},{7,6},{8,7},{9,8},{10,9},{11,1... | collective-permute-start | bytes 15368 | tf_op jit(solution)/shard_map/ppermute | solution.py:19
  134.2 53.2 %collective-permute-start.30 = (f32[10,1,128]{2,1,0:T(1,128)S(1)}, f32[10,1,128]{2,1,0:T(1,128)S(1)}, u32[]{:S(2)}, u32[]{:S(2)}) collective-permute-start(f32[10,1,128]{2,1,0:T(1,128)S(1)} %get-tuple-element.105), channel_id=1, source_target_pairs={{0,1},{1,2},{2,3},{3,4},{4,5},{5,6},{6,7},{7,8},{8,9},{9,10},{10,1... | collective-permute-start | bytes 15368 | tf_op jit(solution)/shard_map/ppermute | solution.py:17
  151.8 39.3 %collective-permute-start.29 = (f32[10,1,128]{2,1,0:T(1,128)S(1)}, f32[10,1,128]{2,1,0:T(1,128)S(1)}, u32[]{:S(2)}, u32[]{:S(2)}) collective-permute-start(f32[10,1,128]{2,1,0:T(1,128)S(1)} %get-tuple-element.107), channel_id=1, source_target_pairs={{1,0},{2,1},{3,2},{4,3},{5,4},{6,5},{7,6},{8,7},{9,8},{10,9},{11,1... | collective-permute-start | bytes 15368 | tf_op jit(solution)/shard_map/ppermute | solution.py:19
  157.8 33.2 %collective-permute-start.31 = (f32[10,1,128]{2,1,0:T(1,128)S(1)}, f32[10,1,128]{2,1,0:T(1,128)S(1)}, u32[]{:S(2)}, u32[]{:S(2)}) collective-permute-start(f32[10,1,128]{2,1,0:T(1,128)S(1)} %get-tuple-element.108), channel_id=1, source_target_pairs={{0,1},{1,2},{2,3},{3,4},{4,5},{5,6},{6,7},{7,8},{8,9},{9,10},{10,1... | collective-permute-start | bytes 15368 | tf_op jit(solution)/shard_map/ppermute | solution.py:17
  185.5 68.1 %collective-permute-start.51 = (f32[1,4,64]{2,1,0:T(4,128)S(1)}, f32[1,4,64]{2,1,0:T(4,128)S(1)}, u32[]{:S(2)}, u32[]{:S(2)}) collective-permute-start(f32[1,4,64]{2,1,0:T(4,128)S(1)} %broadcast.761), channel_id=1, source_target_pairs={{0,16},{16,32},{32,48},{48,64},{64,80},{80,96},{96,112},{1,17},{17... | collective-permute-start | bytes 3080 | tf_op jit(solution)/shard_map/ppermute | solution.py:17
  187.4 43.1 %collective-permute-start.48 = (f32[1,4,64]{2,1,0:T(4,128)S(1)}, f32[1,4,64]{2,1,0:T(4,128)S(1)}, u32[]{:S(2)}, u32[]{:S(2)}) collective-permute-start(f32[1,4,64]{2,1,0:T(4,128)S(1)} %copy-done.17), channel_id=1, source_target_pairs={{16,0},{32,16},{48,32},{64,48},{80,64},{96,80},{112,96},{17,1},{33... | collective-permute-start | bytes 3080 | tf_op jit(solution)/shard_map/ppermute | solution.py:19
  228.4 100.1 %collective-permute-start.73 = (f32[1,2,32]{2,1,0:T(2,128)S(1)}, f32[1,2,32]{2,1,0:T(2,128)S(1)}, u32[]{:S(2)}, u32[]{:S(2)}) collective-permute-start(f32[1,2,32]{2,1,0:T(2,128)S(1)} %broadcast.771), channel_id=1, source_target_pairs={{16,0},{32,16},{48,32},{64,48},{80,64},{96,80},{112,96},{17,1},{33... | collective-permute-start | bytes 776 | tf_op jit(solution)/shard_map/ppermute | solution.py:19
  243.9 36.0 %collective-permute-start.52 = (f32[6,1,64]{2,1,0:T(1,128)S(1)}, f32[6,1,64]{2,1,0:T(1,128)S(1)}, u32[]{:S(2)}, u32[]{:S(2)}) collective-permute-start(f32[6,1,64]{2,1,0:T(1,128)S(1)} %get-tuple-element.162), channel_id=1, source_target_pairs={{1,0},{2,1},{3,2},{4,3},{5,4},{6,5},{7,6},{8,7},{9,8},{10,9},{11,1... | collective-permute-start | bytes 4616 | tf_op jit(solution)/shard_map/ppermute | solution.py:19
  249.5 32.4 %collective-permute-start.54 = (f32[6,1,64]{2,1,0:T(1,128)S(1)}, f32[6,1,64]{2,1,0:T(1,128)S(1)}, u32[]{:S(2)}, u32[]{:S(2)}) collective-permute-start(f32[6,1,64]{2,1,0:T(1,128)S(1)} %get-tuple-element.161), channel_id=1, source_target_pairs={{0,1},{1,2},{2,3},{3,4},{4,5},{5,6},{6,7},{7,8},{8,9},{9,10},{10,1... | collective-permute-start | bytes 4616 | tf_op jit(solution)/shard_map/ppermute | solution.py:17
  266.5 19.1 %collective-permute-start.53 = (f32[6,1,64]{2,1,0:T(1,128)S(1)}, f32[6,1,64]{2,1,0:T(1,128)S(1)}, u32[]{:S(2)}, u32[]{:S(2)}) collective-permute-start(f32[6,1,64]{2,1,0:T(1,128)S(1)} %get-tuple-element.163), channel_id=1, source_target_pairs={{1,0},{2,1},{3,2},{4,3},{5,4},{6,5},{7,6},{8,7},{9,8},{10,9},{11,1... | collective-permute-start | bytes 4616 | tf_op jit(solution)/shard_map/ppermute | solution.py:19
  272.6 15.0 %collective-permute-start.55 = (f32[6,1,64]{2,1,0:T(1,128)S(1)}, f32[6,1,64]{2,1,0:T(1,128)S(1)}, u32[]{:S(2)}, u32[]{:S(2)}) collective-permute-start(f32[6,1,64]{2,1,0:T(1,128)S(1)} %get-tuple-element.164), channel_id=1, source_target_pairs={{0,1},{1,2},{2,3},{3,4},{4,5},{5,6},{6,7},{7,8},{8,9},{9,10},{10,1... | collective-permute-start | bytes 4616 | tf_op jit(solution)/shard_map/ppermute | solution.py:17
  280.0 50.9 %collective-permute-start.75 = (f32[1,2,32]{2,1,0:T(2,128)S(1)}, f32[1,2,32]{2,1,0:T(2,128)S(1)}, u32[]{:S(2)}, u32[]{:S(2)}) collective-permute-start(f32[1,2,32]{2,1,0:T(2,128)S(1)} %broadcast.771), channel_id=1, source_target_pairs={{0,16},{16,32},{32,48},{48,64},{64,80},{80,96},{96,112},{1,17},{17... | collective-permute-start | bytes 776 | tf_op jit(solution)/shard_map/ppermute | solution.py:17
  314.5 47.9 %collective-permute-start.76 = (f32[4,1,32]{2,1,0:T(1,128)S(1)}, f32[4,1,32]{2,1,0:T(1,128)S(1)}, u32[]{:S(2)}, u32[]{:S(2)}) collective-permute-start(f32[4,1,32]{2,1,0:T(1,128)S(1)} %get-tuple-element.242), channel_id=1, source_target_pairs={{1,0},{2,1},{3,2},{4,3},{5,4},{6,5},{7,6},{8,7},{9,8},{10,9},{11,1... | collective-permute-start | bytes 1544 | tf_op jit(solution)/shard_map/ppermute | solution.py:19
  322.9 39.5 %collective-permute-start.78 = (f32[4,1,32]{2,1,0:T(1,128)S(1)}, f32[4,1,32]{2,1,0:T(1,128)S(1)}, u32[]{:S(2)}, u32[]{:S(2)}) collective-permute-start(f32[4,1,32]{2,1,0:T(1,128)S(1)} %get-tuple-element.241), channel_id=1, source_target_pairs={{0,1},{1,2},{2,3},{3,4},{4,5},{5,6},{6,7},{7,8},{8,9},{9,10},{10,1... | collective-permute-start | bytes 1544 | tf_op jit(solution)/shard_map/ppermute | solution.py:17
  (184 other events, 1794.1 us)
where the time goes:
time: 826 us; the launch traced here: 820 us
  starting transfers between devices  505 us (61%)
  waiting for transfers between devices  222 us (27%)
  local copies, waits for them, and re-layouts  59.7 us (7%)
  other arithmetic  29.7 us (4%)
    ppermute x94, starting transfers between devices, extended(): lax.ppermute(tail, axis, [(i, (i + 1) % count) for i in range(ends)])  264 us
    ppermute x94, starting transfers between devices, extended(): lax.ppermute(head, axis, [((i + 1) % count, i) for i in range(ends)])  240 us
    ppermute x94, waiting for transfers between devices, extended(): lax.ppermute(tail, axis, [(i, (i + 1) % count) for i in range(ends)])  222 us
    reshape x4, local copies, waits for them, and re-layouts, coarsen(): blocks = values.reshape(size_x // 2, 2, size_y // 2, 2, size_z // 2, 2)  40 us
    reduce_sum x6, other arithmetic, coarsen(): return blocks.sum(axis=(1, 3, 5)) * 0.125  17.8 us
  transfers between devices with their start and end apart: 188, of which 76 were waited for; matrix products, arithmetic and copies ran while one was open for 10% of the time, Pallas kernels for 0%

commit v1 on v0

v1 whole, which is shorter than its diff:
```python
import jax
import jax.numpy as jnp
from jax import lax
from jax.experimental import pallas as pl
from jax.experimental.pallas import tpu as pltpu
from jax.sharding import PartitionSpec as P

COARSE_SWEEPS = 8
MESH = pl.DeviceIdType.MESH
F32 = jnp.float32
GX, GY = 8, 16
DIRECTIONS = [(-1, 0), (1, 0), (0, -1), (0, 1), (-1, -1), (-1, 1), (1, -1), (1, 1)]
CHIPS = sorted(
    [(x, y, z) for x in range(4) for y in range(4) for z in range(4) if (x, y, z) != (0, 0, 0)],
    key=lambda d: -sum(min(c, 4 - c) for c in d),
)


def iota(shape, dim):
    return lax.broadcasted_iota(jnp.int32, shape, dim)


def roll(values, shift):
    return pltpu.roll(values, shift % 128, values.ndim - 1)


def halo_copies(refs, width, extent, origin, sems, position):
    src, src_origin, dst = refs
    gx, gy = position
    copies = []
    for index, (dx, dy) in enumerate(DIRECTIONS):
        src_at, dst_at = [], []
        for step, size, here, there in zip((dx, dy), extent, src_origin, origin):
            if step == 0:
                src_at.append(slice(here, here + size))
                dst_at.append(slice(there, there + size))
            elif step > 0:
                src_at.append(slice(here + size - width, here + size))
                dst_at.append(slice(there - width, there))
            else:
                src_at.append(slice(here, here + width))
                dst_at.append(slice(there + size, there + size + width))
        lead = (slice(None),) * (len(dst.shape) - 3)
        copies.append(
            pltpu.make_async_remote_copy(
                src_ref=src.at[lead + tuple(src_at)],
                dst_ref=dst.at[lead + tuple(dst_at)],
                send_sem=sems.at[0, index],
                recv_sem=sems.at[1, index],
                device_id=(lax.rem(gx + dx + GX, GX), lax.rem(gy + dy + GY, GY)),
                device_id_type=MESH,
            )
        )
    return copies


def kernel(
    image, conduct, out,
    kx, vx, vs, vk, c0, s0, d0, t0, p0,
    k1, s1x, v1, vk1, c1, s1, i1, d1, t1, p1,
    own2, part2, mix2, kg, sg, v2, c2, s2, i2, d2, t2, p2,
    k3, v3, c3, s3, i3, dummy,
    halo_sems, pair_sems,
):
    gx, gy = lax.axis_index("gx"), lax.axis_index("gy")
    chip_x, core = gx // 2, lax.rem(gx, 2)
    chip_z, chip_y = gy // 4, lax.rem(gy, 4)
    sibling = (chip_x * 2 + 1 - core, gy)
    chips = [
        (lax.rem(chip_x + x, 4) * 2 + core, lax.rem(chip_z + z, 4) * 4 + lax.rem(chip_y + y, 4))
        for x, y, z in CHIPS
    ]
    position = (gx, gy)

    barrier = pltpu.get_barrier_semaphore()
    greeted = chips + [
        (lax.rem(gx + dx + GX, GX), lax.rem(gy + dy + GY, GY)) for dx, dy in DIRECTIONS if dx
    ]
    for peer in greeted:
        pl.semaphore_signal(barrier, inc=1, device_id=peer, device_id_type=MESH)

    lane0 = iota((16, 128), 1)
    odd_row = iota((16, 128), 0) & 1
    low0 = lane0 < 64
    half_lane = (lane0 & 63) * 2

    def split(values, par):
        parity = odd_row ^ par
        first = half_lane + jnp.where(low0, parity, 1 - parity)
        second = half_lane + jnp.where(low0, 1 - parity, parity)
        left = jnp.take_along_axis(values[:, :128], first, axis=1)
        right = jnp.take_along_axis(values[:, 128:], second, axis=1)
        return jnp.where(low0, left, right), roll(jnp.where(low0, right, left), 64)

    def join(red, black, par):
        parity = odd_row ^ par
        turned = roll(black, 64)
        left, right = jnp.where(low0, red, turned), jnp.where(low0, turned, red)
        same = (lane0 & 1) == parity
        half = lane0 >> 1
        first = half + jnp.where(same, 0, 64)
        second = half + jnp.where(same, 64, 0)
        return jnp.take_along_axis(left, first, axis=1), jnp.take_along_axis(right, second, axis=1)

    for i in range(16):
        kx[0, i + 5, 8:24], kx[1, i + 5, 8:24] = split(conduct[i], i & 1)
    for i in range(16):
        red, black = split(image[i], i & 1)
        vx[0, i + 5, 8:24], vx[1, i + 5, 8:24] = red, black
        vs[0, i], vs[1, i] = red, black
    nothing = jnp.zeros((4, 4, 8, 128), F32)
    for ref in (kg, v2):
        ref[:, :, 0:8], ref[:, :, 72:80] = nothing, nothing
    v3[...] = jnp.zeros(v3.shape, F32)
    k3[...] = jnp.zeros(k3.shape, F32)

    pl.semaphore_wait(barrier, len(greeted))

    send_k = halo_copies((kx, (5, 8), kx), 5, (16, 16), (5, 8), halo_sems.at[0], position)
    send_v = halo_copies((vs, (0, 0), vx), 5, (16, 16), (5, 8), halo_sems.at[1], position)
    for copy in send_k + send_v:
        copy.start()

    def block_mean(block):
        for i in range(8):
            t0[i] = block(2 * i) + block(2 * i + 1)
        return [0.125 * (t0[i, pl.ds(0, 8, stride=2)] + t0[i, pl.ds(1, 8, stride=2)]) for i in range(8)]

    even_lane = (iota((8, 128), 1) & 63) * 2

    def block_mean_1(rows):
        for i in range(4):
            pair = rows[2 * i] + rows[2 * i + 1]
            t1[i] = jnp.take_along_axis(pair, even_lane, axis=1) + jnp.take_along_axis(pair, even_lane + 1, axis=1)
        for i in range(4):
            own2[i] = 0.125 * (t1[i, pl.ds(0, 4, stride=2)] + t1[i, pl.ds(1, 4, stride=2)])

    def pair_copy(src, dst, kind, step):
        return pltpu.make_async_remote_copy(
            src_ref=src, dst_ref=dst, send_sem=pair_sems.at[kind, step, 0], recv_sem=pair_sems.at[kind, step, 1],
            device_id=sibling, device_id_type=MESH,
        )

    def gather_copies(kind, whole):
        swap = pair_copy(own2.at[pl.ds(2 - 2 * core, 2)] if kind == 1 else mix2.at[pl.ds(2 - 2 * core, 2)], part2.at[kind], kind, 0)
        rows = (chip_x, pl.ds(2 * core, 2), pl.ds(8 + 4 * gy, 4))
        spread = [
            pltpu.make_async_remote_copy(
                src_ref=mix2.at[pl.ds(4 + 2 * kind, 2)], dst_ref=whole.at[rows], send_sem=pair_sems.at[kind, 1, 0],
                recv_sem=pair_sems.at[kind, 1, 1], device_id=chip, device_id_type=MESH,
            )
            for chip in chips
        ]
        half = whole.at[:, pl.ds(2 * core, 2), 8:72]
        share = pair_copy(half, half, kind, 2)
        return swap, spread, share

    def mix(kind, own_rows, whole):
        mine = iota((2, 4, 128), 2) // 64 == core
        chip_rows = jnp.where(mine, own_rows, part2[kind])
        mix2[4 + 2 * kind:6 + 2 * kind] = chip_rows
        whole[chip_x, pl.ds(2 * core, 2), pl.ds(8 + 4 * gy, 4)] = chip_rows

    def all_arrived(kind):
        pltpu.make_async_copy(dummy, dummy, pair_sems.at[kind, 1, 1]).wait()

    rows = block_mean(lambda i: kx[0, i + 5, 8:24] + kx[1, i + 5, 8:24])
    for i in range(8):
        k1[i + 7, 16:24] = rows[i]
    block_mean_1(rows)
    mix2[0:4] = own2[...]
    send_k1 = halo_copies((k1, (7, 16), k1), 6, (8, 8), (7, 16), halo_sems.at[2], position)
    swap_k, spread_k, share_k = gather_copies(0, kg)
    swap_k.start()
    for copy in send_k1:
        copy.start()

    shape = (2, 24, 128)
    sub, lanes = iota(shape, 1), iota(shape, 2)
    even_row = ((iota(shape, 0) + sub) & 1) == 0
    wy_low = jnp.where((sub == 4) & (gy == 0), 0.0, 0.5).astype(F32)
    wy_high = jnp.where((sub == 19) & (gy == GY - 1), 0.0, 0.5).astype(F32)
    wx_low = jnp.where(gx == 0, 0.0, 0.5).astype(F32)
    wx_high = jnp.where(gx == GX - 1, 0.0, 0.5).astype(F32)
    wz = [
        jnp.where(even_row, jnp.where(lanes == 0, 0.0, 0.5), jnp.where(lanes == 127, 0.0, 0.5)).astype(F32),
        jnp.where(even_row, jnp.where(lanes == 127, 0.0, 0.5), jnp.where(lanes == 0, 0.0, 0.5)).astype(F32),
    ]

    def beside(values, colour, rows_even):
        below, above = roll(values, 1), roll(values, -1)
        return jnp.where(rows_even, below, above) if colour == 0 else jnp.where(rows_even, above, below)

    row_index = iota((2, 1, 1), 0)

    def couplings_0(colour, start, stop):
        for i in range(start, stop, 2):
            e = i + 5
            here, other = kx[colour, e:e + 2, 4:28], kx[1 - colour, e:e + 2, 4:28]
            wx_l = jnp.where(row_index == 0, wx_low, 0.5) if i == 0 else 0.5
            wx_h = jnp.where(row_index == 1, wx_high, 0.5) if i == 14 else 0.5
            parts = [
                (here + kx[1 - colour, e - 1:e + 1, 4:28]) * wx_l,
                (here + kx[1 - colour, e + 1:e + 3, 4:28]) * wx_h,
                (here + kx[1 - colour, e:e + 2, 3:27]) * wy_low,
                (here + kx[1 - colour, e:e + 2, 5:29]) * wy_high,
                (here + other) * 0.5,
                (here + beside(other, colour, even_row)) * wz[colour],
            ]
            total = ((parts[0] + parts[1]) + (parts[2] + parts[3])) + ((parts[4] + parts[5]) + 1.0)
            inverse = 1.0 / total
            d0[colour, i + 4:i + 6] = total
            s0[colour, i + 4:i + 6] = inverse
            for n in range(6):
                c0[colour, n, i + 4:i + 6] = parts[n] * inverse

    def update_0(colour, i, lo, hi, rows_even):
        e, f = i + 5, i + 4
        a, b = lo + 8, hi + 8
        here = slice(lo + 4, hi + 4)
        other = vx[1 - colour, e:e + 2, a:b]
        acc0 = s0[colour, f:f + 2, here] + c0[colour, 0, f:f + 2, here] * vx[1 - colour, e - 1:e + 1, a:b]
        acc1 = c0[colour, 1, f:f + 2, here] * vx[1 - colour, e + 1:e + 3, a:b]
        acc1 += c0[colour, 2, f:f + 2, here] * vx[1 - colour, e:e + 2, a - 1:b - 1]
        acc2 = c0[colour, 3, f:f + 2, here] * vx[1 - colour, e:e + 2, a + 1:b + 1]
        acc2 += c0[colour, 4, f:f + 2, here] * other
        acc3 = c0[colour, 5, f:f + 2, here] * beside(other, colour, rows_even)
        return (acc0 + acc1) + (acc2 + acc3)

    own_even = ((iota((2, 16, 128), 0) + iota((2, 16, 128), 1)) & 1) == 0

    def half_sweep_0(colour, start, stop, lo=-4, hi=20):
        rows_even = even_row if hi - lo == 24 else own_even
        for i in range(start, stop, 2):
            vx[colour, i + 5:i + 7, lo + 8:hi + 8] = update_0(colour, i, lo, hi, rows_even)

    for copy in send_k:
        copy.wait_recv()
    couplings_0(0, -4, 20)
    couplings_0(1, -4, 20)

    swap_k.wait_recv()
    mix(0, mix2[pl.ds(2 * core, 2)], kg)
    for copy in spread_k:
        copy.start()

    for copy in send_v:
        copy.wait_recv()
    for colour in (0, 1):
        for i in range(-4, 20, 2):
            s0[colour, i + 4:i + 6] = s0[colour, i + 4:i + 6] * vx[colour, i + 5:i + 7, 4:28]

    half_sweep_0(0, -4, 20)
    half_sweep_0(1, -4, 20)
    half_sweep_0(0, -2, 18)
    half_sweep_0(1, -2, 18)

    def residual_0(i):
        total = None
        for colour in (0, 1):
            left = update_0(colour, i, 0, 16, own_even) - vx[colour, i + 5:i + 7, 8:24]
            left = d0[colour, i + 4:i + 6, 4:20] * left
            total = left if total is None else total + left
        return total

    for i in range(8):
        both = residual_0(2 * i)
        t0[i] = both[0] + both[1]
    for i in range(8):
        s1x[i + 7, 16:24] = 0.125 * (t0[i, pl.ds(0, 8, stride=2)] + t0[i, pl.ds(1, 8, stride=2)])
    send_s1 = halo_copies((s1x, (7, 16), s1x), 5, (8, 8), (7, 16), halo_sems.at[3], position)
    for copy in send_s1:
        copy.start()
    vk[5:21, 8:24] = vx[1, 5:21, 8:24]
    send_vk = halo_copies((vk, (5, 8), vk), 4, (16, 16), (5, 8), halo_sems.at[4], position)
    for copy in send_vk:
        copy.start()

    shape = (2, 24, 128)
    col, lanes = iota(shape, 1) - 6, iota(shape, 2)
    w1 = 0.5 / 4.0
    wy_low = jnp.where((col == 0) & (gy == 0), 0.0, w1).astype(F32)
    wy_high = jnp.where((col == 7) & (gy == GY - 1), 0.0, w1).astype(F32)
    wx_low = jnp.where(gx == 0, 0.0, w1).astype(F32)
    wx_high = jnp.where(gx == GX - 1, 0.0, w1).astype(F32)
    wz_low = jnp.where(lanes == 0, 0.0, w1).astype(F32)
    wz_high = jnp.where(lanes == 127, 0.0, w1).astype(F32)

    for copy in send_k1:
        copy.wait_recv()
    for i in range(-6, 14, 2):
        e, f = i + 7, i + 6
        here = k1[e:e + 2, 10:34]
        wx_l = jnp.where(row_index == 0, wx_low, w1) if i == 0 else w1
        wx_h = jnp.where(row_index == 1, wx_high, w1) if i == 6 else w1
        parts = [
            (here + k1[e - 1:e + 1, 10:34]) * wx_l,
            (here + k1[e + 1:e + 3, 10:34]) * wx_h,
            (here + k1[e:e + 2, 9:33]) * wy_low,
            (here + k1[e:e + 2, 11:35]) * wy_high,
            (here + roll(here, 1)) * wz_low,
            (here + roll(here, -1)) * wz_high,
        ]
        total = ((parts[0] + parts[1]) + (parts[2] + parts[3])) + ((parts[4] + parts[5]) + 1.0)
        inverse = 1.0 / total
        d1[f:f + 2] = total
        i1[f:f + 2] = inverse
        for n in range(6):
            c1[n, f:f + 2] = parts[n] * inverse

    def update_1(i, lo, hi):
        e, f = i + 7, i + 6
        a, b = lo + 16, hi + 16
        here = slice(lo + 6, hi + 6)
        mid = v1[e:e + 2, a:b]
        acc0 = s1[f:f + 2, here] + c1[0, f:f + 2, here] * v1[e - 1:e + 1, a:b]
        acc1 = c1[1, f:f + 2, here] * v1[e + 1:e + 3, a:b] + c1[2, f:f + 2, here] * v1[e:e + 2, a - 1:b - 1]
        acc2 = c1[3, f:f + 2, here] * v1[e:e + 2, a + 1:b + 1] + c1[4, f:f + 2, here] * roll(mid, 1)
        acc3 = c1[5, f:f + 2, here] * roll(mid, -1)
        return (acc0 + acc1) + (acc2 + acc3), mid

    def colour_1(size):
        box = (2, size, 128)
        return (iota(box, 0) + iota(box, 1) + iota(box, 2)) & 1

    colours_24, colours_16 = colour_1(24), colour_1(16)

    def half_sweep_1(colour, start, stop, lo, hi):
        colours = colours_24 if hi - lo == 24 else colours_16
        for i in range(start, stop, 2):
            new, old = update_1(i, lo, hi)
            v1[i + 7:i + 9, lo + 16:hi + 16] = jnp.where(colours == colour, new, old)

    lane = iota((64, 128), 1)
    place = lane & 63
    j_row = iota((64, 128), 0)
    low = lane < 64
    w2 = 0.5 / 16.0
    wy_low = jnp.where(j_row == 0, 0.0, w2).astype(F32)
    wy_high = jnp.where(j_row == 63, 0.0, w2).astype(F32)
    wz_low = jnp.where(place == 0, 0.0, w2).astype(F32)
    wz_high = jnp.where(place == 63, 0.0, w2).astype(F32)
    first_x = jnp.where(low, 0.0, w2).astype(F32)
    last_x = jnp.where(low, w2, 0.0).astype(F32)

    def row_before(ref, x, i, last, at, first_half):
        if i > 0:
            return ref[x, i - 1, at]
        return roll(jnp.where(first_half, ref[x, last, at], ref[(x + 3) % 4, last, at]), 64)

    def row_after(ref, x, i, last, at, first_half):
        if i < last:
            return ref[x, i + 1, at]
        return roll(jnp.where(first_half, ref[(x + 1) % 4, 0, at], ref[x, 0, at]), 64)

    all_arrived(0)
    share_k.start()
    share_k.wait_recv()
    at = slice(8, 72)
    for x in range(4):
        for i in range(4):
            here = kg[x, i, at]
            parts = [
                (here + row_before(kg, x, i, 3, at, low)) * (first_x if x == 0 and i == 0 else w2),
                (here + row_after(kg, x, i, 3, at, low)) * (last_x if x == 3 and i == 3 else w2),
                (here + kg[x, i, 7:71]) * wy_low,
                (here + kg[x, i, 9:73]) * wy_high,
                (here + roll(here, 1)) * wz_low,
                (here + roll(here, -1)) * wz_high,
            ]
            total = ((parts[0] + parts[1]) + (parts[2] + parts[3])) + ((parts[4] + parts[5]) + 1.0)
            inverse = 1.0 / total
            d2[x, i] = total
            i2[x, i] = inverse
            for n in range(6):
                c2[n, x, i, at] = parts[n] * inverse

    even_place = (lane & 1) == 0

    def pair_lanes(values):
        return values + jnp.where(even_place, roll(values, -1), roll(values, 1))

    def block_mean_2(x, i):
        return 0.125 * (t2[x, i, pl.ds(0, 32, stride=2)] + t2[x, i, pl.ds(1, 32, stride=2)])

    for x in range(4):
        for i in range(2):
            t2[x, i] = pair_lanes(kg[x, 2 * i, at] + kg[x, 2 * i + 1, at])
    for x in range(4):
        for i in range(2):
            k3[x, i, 8:40] = block_mean_2(x, i)
    lane3 = iota((32, 128), 1)
    place3 = (lane3 & 63) >> 1
    row3 = iota((32, 128), 0)
    low3 = lane3 < 64
    w3 = 0.5 / 64.0
    wy_low = jnp.where(row3 == 0, 0.0, w3).astype(F32)
    wy_high = jnp.where(row3 == 31, 0.0, w3).astype(F32)
    wz_low = jnp.where(place3 == 0, 0.0, w3).astype(F32)
    wz_high = jnp.where(place3 == 31, 0.0, w3).astype(F32)
    first_x = jnp.where(low3, 0.0, w3).astype(F32)
    last_x = jnp.where(low3, w3, 0.0).astype(F32)
    at3 = slice(8, 40)
    for x in range(4):
        for i in range(2):
            here = k3[x, i, at3]
            parts = [
                (here + row_before(k3, x, i, 1, at3, low3)) * (first_x if x == 0 and i == 0 else w3),
                (here + row_after(k3, x, i, 1, at3, low3)) * (last_x if x == 3 and i == 1 else w3),
                (here + k3[x, i, 7:39]) * wy_low,
                (here + k3[x, i, 9:41]) * wy_high,
                (here + roll(here, 2)) * wz_low,
                (here + roll(here, -2)) * wz_high,
            ]
            total = ((parts[0] + parts[1]) + (parts[2] + parts[3])) + ((parts[4] + parts[5]) + 1.0)
            inverse = 1.0 / total
            i3[x, i] = inverse
            for n in range(6):
                c3[n, x, i] = parts[n] * inverse

    for copy in send_s1:
        copy.wait_recv()
    for i in range(-6, 14, 2):
        s1[i + 6:i + 8] = i1[i + 6:i + 8] * s1x[i + 7:i + 9, 10:34]
    for i in range(-4, 12, 2):
        v1[i + 7:i + 9, 12:28] = jnp.where(colours_16 == 0, s1[i + 6:i + 8, 2:18], 0.0)
    half_sweep_1(1, -4, 12, -4, 12)
    half_sweep_1(0, -2, 10, -4, 12)
    half_sweep_1(1, -2, 10, -4, 12)
    rows = []
    for i in range(0, 8, 2):
        new, old = update_1(i, 0, 8)
        left = d1[i + 6:i + 8, 6:14] * (new - old)
        rows += [left[0], left[1]]
    block_mean_1(rows)
    swap_s, spread_s, share_s = gather_copies(1, sg)
    swap_s.start()
    vk1[7:15, 16:24] = v1[7:15, 16:24]
    send_vk1 = halo_copies((vk1, (7, 16), vk1), 6, (8, 8), (7, 16), halo_sems.at[5], position)
    swap_s.wait_recv()
    mix(1, own2[pl.ds(2 * core, 2)], sg)
    for copy in spread_s:
        copy.start()
    for copy in send_vk1:
        copy.start()
    all_arrived(1)
    share_s.start()
    share_s.wait_recv()

    colours_2 = [(i + j_row + place) & 1 for i in range(2)]
    for x in range(4):
        for i in range(4):
            source = i2[x, i] * sg[x, i, at]
            s2[x, i, at] = source
            v2[x, i, at] = jnp.where(colours_2[i & 1] == 0, source, 0.0)

    def update_2(x, i, at, before, after, first_half):
        mid = v2[x, i, at]
        acc0 = s2[x, i, at] + c2[0, x, i, at] * row_before(v2, x, i, 3, at, first_half)
        acc1 = c2[1, x, i, at] * row_after(v2, x, i, 3, at, first_half) + c2[2, x, i, at] * v2[x, i, before]
        acc2 = c2[3, x, i, at] * v2[x, i, after] + c2[4, x, i, at] * roll(mid, 1)
        acc3 = c2[5, x, i, at] * roll(mid, -1)
        return (acc0 + acc1) + (acc2 + acc3), mid

    def half_sweep_2(colour):
        for x in range(4):
            for i in range(4):
                new, old = update_2(x, i, at, slice(7, 71), slice(9, 73), low)
                v2[x, i, at] = jnp.where(colours_2[i & 1] == colour, new, old)

    half_sweep_2(1)
    half_sweep_2(0)
    half_sweep_2(1)
    for x in range(4):
        for i in range(2):
            total = None
            for n in (2 * i, 2 * i + 1):
                new, old = update_2(x, n, at, slice(7, 71), slice(9, 73), low)
                left = d2[x, n] * (new - old)
                total = left if total is None else total + left
            t2[x, i] = pair_lanes(total)
    for x in range(4):
        for i in range(2):
            s3[x, i] = i3[x, i] * block_mean_2(x, i)

    colours_3 = [(i + row3 + place3) & 1 for i in range(2)]

    def half_sweep_3(colour):
        for x in range(4):
            for i in range(2):
                mid = v3[x, i, at3]
                acc0 = s3[x, i] + c3[0, x, i] * row_before(v3, x, i, 1, at3, low3)
                acc1 = c3[1, x, i] * row_after(v3, x, i, 1, at3, low3) + c3[2, x, i] * v3[x, i, 7:39]
                acc2 = c3[3, x, i] * v3[x, i, 9:41] + c3[4, x, i] * roll(mid, 2)
                acc3 = c3[5, x, i] * roll(mid, -2)
                new = (acc0 + acc1) + (acc2 + acc3)
                v3[x, i, at3] = jnp.where(colours_3[i] == colour, new, mid)

    def sweep_3(_, carry):
        half_sweep_3(0)
        half_sweep_3(1)
        return carry

    lax.fori_loop(0, COARSE_SWEEPS, sweep_3, 0)

    for x in range(4):
        for i in range(2):
            p2[x, i, pl.ds(8, 32, stride=2)] = v3[x, i, at3]
            p2[x, i, pl.ds(9, 32, stride=2)] = v3[x, i, at3]
    strip = gy // 2
    strip = pl.multiple_of(8 * (strip + 1 - (strip + 7) // 8 - (strip + 1) // 8), 8)
    at, before, after = pl.ds(strip, 24), pl.ds(strip - 1, 24), pl.ds(strip + 1, 24)
    xs = [lax.rem(chip_x + n, 4) for n in (3, 0, 1)]
    low = iota((24, 128), 1) < 64
    place = iota((24, 128), 1) & 63
    colours_2 = [(i + iota((24, 128), 0) + place) & 1 for i in range(2)]
    for x in xs:
        for i in range(4):
            v2[x, i, at] = v2[x, i, at] + p2[x, i // 2, at]
    for colour in (0, 1, 0, 1):
        for x in xs:
            for i in range(4):
                new, old = update_2(x, i, at, before, after, low)
                v2[x, i, at] = jnp.where(colours_2[i & 1] == colour, new, old)

    spot = iota((10, 128), 1) >> 1
    for d in range(-3, 7):
        row = 4 * core + d + 8
        x = lax.rem(chip_x + 3 + row // 8, 4)
        where = spot + 64 * (lax.rem(row, 8) // 4)
        coarse = jnp.take_along_axis(v2[x, d % 4, pl.ds(4 * gy + 5, 10)], where, axis=1)
        p1[d + 3, pl.ds(0, 10, stride=2)] = coarse
        p1[d + 3, pl.ds(1, 10, stride=2)] = coarse
    for copy in send_vk1:
        copy.wait_recv()
    for i in range(-6, 14):
        v1[i + 7, 10:30] = vk1[i + 7, 10:30] + p1[i // 2 + 3]
    half_sweep_1(0, -6, 14, -6, 18)
    half_sweep_1(1, -4, 12, -4, 12)
    half_sweep_1(0, -4, 12, -4, 12)
    half_sweep_1(1, -2, 10, -4, 12)

    for i in range(-2, 10):
        p0[i + 2, pl.ds(0, 12, stride=2)] = v1[i + 7, 14:26]
        p0[i + 2, pl.ds(1, 12, stride=2)] = v1[i + 7, 14:26]
    for copy in send_vk:
        copy.wait_recv()
    for i in range(-4, 20):
        vx[1, i + 5, 4:28] = vk[i + 5, 4:28] + p0[i // 2 + 2]
    half_sweep_0(0, -4, 20)
    half_sweep_0(1, -2, 18)
    half_sweep_0(0, -2, 18)
    half_sweep_0(1, 0, 16, 0, 16)
    for i in range(16):
        out[i, :, :128], out[i, :, 128:] = join(vx[0, i + 5, 8:24], vx[1, i + 5, 8:24], i & 1)

    for copy in send_k + send_v + send_k1 + send_s1 + send_vk + send_vk1 + [swap_k, share_k, swap_s, share_s]:
        copy.wait_send()
    for kind in (0, 1):
        pltpu.make_async_copy(dummy, dummy, pair_sems.at[kind, 1, 0]).wait()


def v_cycle(image, conduct):
    def vmem(*shape):
        return pltpu.VMEM(shape, F32)

    frame0, frame1, frame2 = (26, 32, 128), (22, 40, 128), (4, 4, 80, 128)
    return pl.pallas_call(
        kernel,
        out_shape=jax.ShapeDtypeStruct((16, 16, 256), F32),
        in_specs=[pl.BlockSpec(memory_space=pltpu.VMEM)] * 2,
        out_specs=pl.BlockSpec(memory_space=pltpu.VMEM),
        scratch_shapes=[
            vmem(2, *frame0), vmem(2, *frame0), vmem(2, 16, 16, 128), vmem(*frame0), vmem(2, 6, 24, 24, 128),
            vmem(2, 24, 24, 128), vmem(2, 24, 24, 128), vmem(8, 16, 128), vmem(12, 24, 128),
            vmem(*frame1), vmem(*frame1), vmem(*frame1), vmem(*frame1), vmem(6, 20, 24, 128), vmem(20, 24, 128),
            vmem(20, 24, 128), vmem(20, 24, 128), vmem(4, 8, 128), vmem(10, 20, 128),
            vmem(4, 4, 128), vmem(2, 2, 4, 128), vmem(8, 4, 128), vmem(*frame2), vmem(*frame2), vmem(*frame2),
            vmem(6, *frame2), vmem(*frame2), vmem(4, 4, 64, 128), vmem(4, 4, 64, 128), vmem(4, 2, 64, 128),
            vmem(4, 2, 80, 128),
            vmem(4, 2, 48, 128), vmem(4, 2, 48, 128), vmem(6, 4, 2, 32, 128), vmem(4, 2, 32, 128),
            vmem(4, 2, 32, 128), vmem(63, 2, 4, 128),
            pltpu.SemaphoreType.DMA((6, 2, 8)), pltpu.SemaphoreType.DMA((2, 3, 2)),
        ],
        compiler_params=pltpu.CompilerParams(
            collective_id=0, has_side_effects=True, vmem_limit_bytes=48 * 2**20
        ),
        name="v_cycle",
    )(image, conduct)


def solution(mesh):
    return jax.shard_map(
        v_cycle,
        mesh=mesh,
        in_specs=(P("gx", "gy", None), P("gx", "gy", None)),
        out_specs=P("gx", "gy", None),
        check_vma=False,
    )
```

time: 826 us -> 56.5 us (0.07)
  the two profiles are of different devices: /device:TPU:100 before, /device:TPU:1 now
where the time goes in v1:
time: 56.5 us; the launch traced here: 56.3 us
  Pallas kernels  53.7 us (95%)
  local copies, waits for them, and re-layouts  2.6 us (5%)
    pallas_call x1, Pallas kernels, v_cycle(): pl.pallas_call(kernel, out_shape=jax.ShapeDtypeStruct((16, 16, 256), F32)...  53.7 us
    unnamed x5, local copies, waits for them, and re-layouts  2.6 us

profile of v1, /device:TPU:1, one launch (start us, length us, event | category | flops | bytes accessed | tf_op | source)
XLA Modules:
  0.0 56.3 jit_solution(403547047584310174)
XLA Ops:
  0.0 0.0 copy-start
  0.0 0.9 %copy-done = f32[16,16,256]{2,1,0:T(8,128)S(1)} copy-done((f32[16,16,256]{2,1,0:T(8,128)S(1)}, f32[16,16,256]{2,1,0:T(8,128)}, u32[]{:S(2)}) %copy-start) | copy-done | bytes 262168
  1.0 0.0 copy-start.1
  1.0 0.9 %copy-done.1 = f32[16,16,256]{2,1,0:T(8,128)S(1)} copy-done((f32[16,16,256]{2,1,0:T(8,128)S(1)}, f32[16,16,256]{2,1,0:T(8,128)}, u32[]{:S(2)}) %copy-start.1) | copy-done | bytes 262168
  1.9 53.7 %v_cycle.1 = f32[16,16,256]{2,1,0:T(8,128)S(1)} custom-call(f32[16,16,256]{2,1,0:T(8,128)S(1)} %copy-done, f32[16,16,256]{2,1,0:T(8,128)S(1)} %copy-done.1), custom_call_target="tpu_custom_call" | custom-call | tf_op jit(solution)/shard_map/v_cycle/pallas_call | solution.py:568
  55.6 0.7 %copy.4 = f32[16,16,256]{2,1,0:T(8,128)} copy(f32[16,16,256]{2,1,0:T(8,128)S(1)} %v_cycle.1) | data formatting | bytes 524288
Async XLA Ops:
  0.0 0.9 %copy-start = (f32[16,16,256]{2,1,0:T(8,128)S(1)}, f32[16,16,256]{2,1,0:T(8,128)}, u32[]{:S(2)}) copy-start(f32[16,16,256]{2,1,0:T(8,128)} %image.1) | copy-start | bytes 786436
  1.0 0.9 %copy-start.1 = (f32[16,16,256]{2,1,0:T(8,128)S(1)}, f32[16,16,256]{2,1,0:T(8,128)}, u32[]{:S(2)}) copy-start(f32[16,16,256]{2,1,0:T(8,128)} %conduct.1) | copy-start | bytes 786436

commit v2 on v1

v2 whole, which is shorter than its diff:
```python
import jax
import jax.numpy as jnp
from jax import lax
from jax.experimental import pallas as pl
from jax.experimental.pallas import tpu as pltpu
from jax.sharding import PartitionSpec as P

COARSE_SWEEPS = 8
MESH = pl.DeviceIdType.MESH
F32 = jnp.float32
GX, GY = 8, 16
DIRECTIONS = [(-1, 0), (1, 0), (0, -1), (0, 1), (-1, -1), (-1, 1), (1, -1), (1, 1)]
CHIPS = sorted(
    [(x, y, z) for x in range(4) for y in range(4) for z in range(4) if (x, y, z) != (0, 0, 0)],
    key=lambda d: -sum(min(c, 4 - c) for c in d),
)


def iota(shape, dim):
    return lax.broadcasted_iota(jnp.int32, shape, dim)


def roll(values, shift):
    return pltpu.roll(values, shift % 128, values.ndim - 1)


def halo_copies(src, src_origin, dst, origin, extent, widths, sems, position, corners=None):
    gx, gy = position
    lead = (slice(None),) * (len(dst.shape) - 3)

    def piece(step, size, here, there, start, stop):
        if step == 0:
            return slice(here, here + size), slice(there, there + size)
        if step > 0:
            return slice(here + size - stop, here + size - start), slice(there - stop, there - start)
        return slice(here + start, here + stop), slice(there + size + start, there + size + stop)

    copies = []
    for dx, dy in DIRECTIONS:
        boxes = [((0, widths[0]), (0, widths[1]))]
        if dx and dy and corners is not None:
            boxes = [((start, stop), (0, width)) for start, stop, width in corners]
        for box_x, box_y in boxes:
            src_x, dst_x = piece(dx, extent[0], src_origin[0], origin[0], *box_x)
            src_y, dst_y = piece(dy, extent[1], src_origin[1], origin[1], *box_y)
            copies.append(
                pltpu.make_async_remote_copy(
                    src_ref=src.at[lead + (src_x, src_y)],
                    dst_ref=dst.at[lead + (dst_x, dst_y)],
                    send_sem=sems.at[0, len(copies)],
                    recv_sem=sems.at[1, len(copies)],
                    device_id=(lax.rem(gx + dx + GX, GX), lax.rem(gy + dy + GY, GY)),
                    device_id_type=MESH,
                )
            )
    return copies


def couple(here, same, cross, low, high, other, weights, z_step):
    w, w_cross, w_low, w_high, w_below, w_above = weights
    parts = [
        (here + same) * w,
        (here + cross) * w_cross,
        (here + low) * w_low,
        (here + high) * w_high,
        (here + roll(other, z_step)) * w_below,
        (here + roll(other, -z_step)) * w_above,
    ]
    total = ((parts[0] + parts[1]) + (parts[2] + parts[3])) + ((parts[4] + parts[5]) + 1.0)
    inverse = 1.0 / total
    return [part * inverse for part in parts], total, inverse


def relax(source, couplings, same, cross, low, high, z_step):
    acc0 = source + couplings[0] * same
    acc1 = couplings[4] * roll(same, z_step) + couplings[5] * roll(same, -z_step)
    acc2 = couplings[2] * low + couplings[3] * high
    return (acc0 + acc2) + (acc1 + couplings[1] * cross)


def kernel(
    image, conduct, out,
    image_in, conduct_in, kx, vx, vs, vk, c0, s0, d0, t0, p0,
    k1, s1x, v1, vk1, c1, s1, i1, d1, t1, p1,
    own2, part2, mix2, kg, sg, v2, c2, s2, i2, d2, t2, p2,
    k3, v3, c3, s3, i3, dummy,
    halo_sems, pair_sems, in_sems,
):
    gx, gy = lax.axis_index("gx"), lax.axis_index("gy")
    chip_x, core = gx // 2, lax.rem(gx, 2)
    chip_z, chip_y = gy // 4, lax.rem(gy, 4)
    sibling = (chip_x * 2 + 1 - core, gy)
    chips = [
        (lax.rem(chip_x + x, 4) * 2 + core, lax.rem(chip_z + z, 4) * 4 + lax.rem(chip_y + y, 4))
        for x, y, z in CHIPS
    ]
    position = (gx, gy)
    barrier = pltpu.get_barrier_semaphore()
    greeted = chips + [
        (lax.rem(gx + dx + GX, GX), lax.rem(gy + dy + GY, GY)) for dx, dy in DIRECTIONS if dx
    ]
    fetch_k = pltpu.make_async_copy(conduct, conduct_in, in_sems.at[0])
    fetch_v = pltpu.make_async_copy(image, image_in, in_sems.at[1])
    fetch_k.start()
    fetch_v.start()
    for peer in greeted:
        pl.semaphore_signal(barrier, inc=1, device_id=peer, device_id_type=MESH)

    lane0 = iota((16, 128), 1)
    odd_row = iota((16, 128), 0) & 1
    low0 = lane0 < 64
    half_lane = (lane0 & 63) * 2

    def split(values, par):
        parity = odd_row ^ par
        first = half_lane + jnp.where(low0, parity, 1 - parity)
        second = half_lane + jnp.where(low0, 1 - parity, parity)
        left = jnp.take_along_axis(values[:, :128], first, axis=1)
        right = jnp.take_along_axis(values[:, 128:], second, axis=1)
        return jnp.where(low0, left, right), roll(jnp.where(low0, right, left), 64)

    def join(red, black, par):
        parity = odd_row ^ par
        turned = roll(black, 64)
        left, right = jnp.where(low0, red, turned), jnp.where(low0, turned, red)
        same = (lane0 & 1) == parity
        half = lane0 >> 1
        first = half + jnp.where(same, 0, 64)
        second = half + jnp.where(same, 64, 0)
        return jnp.take_along_axis(left, first, axis=1), jnp.take_along_axis(right, second, axis=1)
    nothing = jnp.zeros((2, 4, 2, 8, 128), F32)
    for ref in (kg, v2):
        ref[:, :, :, 0:8], ref[:, :, :, 72:80] = nothing, nothing
    nothing = jnp.zeros((2, 4, 8, 128), F32)
    for ref in (k3, v3):
        ref[:, :, 0:8], ref[:, :, 40:48] = nothing, nothing
    fetch_k.wait()
    for i in range(16):
        kx[0, i + 5, 8:24], kx[1, i + 5, 8:24] = split(conduct_in[i], i & 1)
    pl.semaphore_wait(barrier, len(greeted))
    cone = [(0, 2, 4), (2, 4, 2)]
    send_k = halo_copies(kx, (5, 8), kx, (5, 8), (16, 16), (5, 5), halo_sems.at[0], position, cone)
    send_v = halo_copies(vs, (0, 0), vx, (5, 8), (16, 16), (5, 5), halo_sems.at[1], position, cone)
    for copy in send_k:
        copy.start()
    fetch_v.wait()
    for i in range(16):
        red, black = split(image_in[i], i & 1)
        vx[0, i + 5, 8:24], vx[1, i + 5, 8:24] = red, black
        vs[0, i], vs[1, i] = red, black
    for copy in send_v:
        copy.start()
    def block_mean():
        return [0.125 * (t0[i, pl.ds(0, 8, stride=2)] + t0[i, pl.ds(1, 8, stride=2)]) for i in range(8)]

    odd_8 = ((iota((8, 128), 0) + iota((8, 128), 1)) & 1) == 1
    odd_4 = ((iota((4, 128), 0) + iota((4, 128), 1)) & 1) == 1
    even_lane = (iota((8, 128), 1) & 63) * 2

    def merge(first, second, odd):
        return jnp.where(odd, second, first), jnp.where(odd, first, second)

    def level_2_share(kind, pairs):
        for i in range(4):
            t1[i] = jnp.take_along_axis(pairs[i], even_lane, axis=1) + jnp.take_along_axis(pairs[i], even_lane + 1, axis=1)
        rows = [0.125 * (t1[i, pl.ds(0, 4, stride=2)] + t1[i, pl.ds(1, 4, stride=2)]) for i in range(4)]
        for a in range(2):
            own2[kind, 0, a], own2[kind, 1, a] = merge(rows[2 * a], rows[2 * a + 1], odd_4)

    def pair_copy(src, dst, kind, step):
        return pltpu.make_async_remote_copy(
            src_ref=src, dst_ref=dst, send_sem=pair_sems.at[kind, step, 0], recv_sem=pair_sems.at[kind, step, 1],
            device_id=sibling, device_id_type=MESH,
        )

    def gather_copies(kind, whole):
        swap = pair_copy(own2.at[kind, 1 - core], part2.at[kind], kind, 0)
        place = (core, chip_x, slice(None), pl.ds(8 + 4 * gy, 4))
        spread = [
            pltpu.make_async_remote_copy(
                src_ref=mix2.at[kind], dst_ref=whole.at[place], send_sem=pair_sems.at[kind, 1 + x, 0],
                recv_sem=pair_sems.at[kind, 1 + x, 1], device_id=chip, device_id_type=MESH,
            )
            for chip, (x, _, _) in zip(chips, CHIPS)
        ]
        planes = [whole.at[core, lax.rem(chip_x + 4 - x, 4), :, 8:72] for x in range(4)]
        share = [pair_copy(plane, plane, kind, 5 + x) for x, plane in enumerate(planes)]
        return swap, spread, share

    def mix(kind, whole):
        mine = iota((2, 4, 128), 2) // 64 == core
        cells = jnp.where(mine, own2[kind, core], part2[kind])
        mix2[kind] = cells
        whole[core, chip_x, :, pl.ds(8 + 4 * gy, 4)] = cells

    def landed(kind, x, which):
        some = dummy.at[0:15] if x == 0 else dummy
        pltpu.make_async_copy(some, some, pair_sems.at[kind, 1 + x, which]).wait()

    def pass_on(kind, share):
        for x in (0, 1, 3, 2):
            landed(kind, x, 1)
            share[x].start()
        for copy in share:
            copy.wait_recv()

    for i in range(8):
        e = 2 * i + 5
        t0[i] = (kx[0, e, 8:24] + kx[1, e, 8:24]) + (kx[0, e + 1, 8:24] + kx[1, e + 1, 8:24])
    rows = block_mean()
    for a in range(4):
        k1[0, a + 4, 16:24], k1[1, a + 4, 16:24] = merge(rows[2 * a], rows[2 * a + 1], odd_8)
    level_2_share(0, [rows[2 * a] + rows[2 * a + 1] for a in range(4)])
    send_k1 = halo_copies(k1, (4, 16), k1, (4, 16), (4, 8), (3, 6), halo_sems.at[2], position)
    swap_k, spread_k, share_k = gather_copies(0, kg)
    swap_k.start()
    for copy in send_k1:
        copy.start()

    shape = (2, 24, 128)
    sub, lanes = iota(shape, 1), iota(shape, 2)
    even_row = ((iota(shape, 0) + sub) & 1) == 0
    wy_low = jnp.where((sub == 4) & (gy == 0), 0.0, 0.5).astype(F32)
    wy_high = jnp.where((sub == 19) & (gy == GY - 1), 0.0, 0.5).astype(F32)
    wx_low = jnp.where(gx == 0, 0.0, 0.5).astype(F32)
    wx_high = jnp.where(gx == GX - 1, 0.0, 0.5).astype(F32)
    wz = [
        jnp.where(even_row, jnp.where(lanes == 0, 0.0, 0.5), jnp.where(lanes == 127, 0.0, 0.5)).astype(F32),
        jnp.where(even_row, jnp.where(lanes == 127, 0.0, 0.5), jnp.where(lanes == 0, 0.0, 0.5)).astype(F32),
    ]

    def beside(values, colour, rows_even):
        below, above = roll(values, 1), roll(values, -1)
        return jnp.where(rows_even, below, above) if colour == 0 else jnp.where(rows_even, above, below)

    row_index = iota((2, 1, 1), 0)

    def couplings_0(colour, start, stop):
        for i in range(start, stop, 2):
            e = i + 5
            here, other = kx[colour, e:e + 2, 4:28], kx[1 - colour, e:e + 2, 4:28]
            wx_l = jnp.where(row_index == 0, wx_low, 0.5) if i == 0 else 0.5
            wx_h = jnp.where(row_index == 1, wx_high, 0.5) if i == 14 else 0.5
            parts = [
                (here + kx[1 - colour, e - 1:e + 1, 4:28]) * wx_l,
                (here + kx[1 - colour, e + 1:e + 3, 4:28]) * wx_h,
                (here + kx[1 - colour, e:e + 2, 3:27]) * wy_low,
                (here + kx[1 - colour, e:e + 2, 5:29]) * wy_high,
                (here + other) * 0.5,
                (here + beside(other, colour, even_row)) * wz[colour],
            ]
            total = ((parts[0] + parts[1]) + (parts[2] + parts[3])) + ((parts[4] + parts[5]) + 1.0)
            inverse = 1.0 / total
            d0[colour, i + 4:i + 6] = total
            s0[colour, i + 4:i + 6] = inverse
            for n in range(6):
                c0[colour, n, i + 4:i + 6] = parts[n] * inverse

    def update_0(colour, i, lo, hi, rows_even):
        e, f = i + 5, i + 4
        a, b = lo + 8, hi + 8
        here = slice(lo + 4, hi + 4)
        other = vx[1 - colour, e:e + 2, a:b]
        acc0 = s0[colour, f:f + 2, here] + c0[colour, 0, f:f + 2, here] * vx[1 - colour, e - 1:e + 1, a:b]
        acc1 = c0[colour, 1, f:f + 2, here] * vx[1 - colour, e + 1:e + 3, a:b]
        acc1 += c0[colour, 2, f:f + 2, here] * vx[1 - colour, e:e + 2, a - 1:b - 1]
        acc2 = c0[colour, 3, f:f + 2, here] * vx[1 - colour, e:e + 2, a + 1:b + 1]
        acc2 += c0[colour, 4, f:f + 2, here] * other
        acc3 = c0[colour, 5, f:f + 2, here] * beside(other, colour, rows_even)
        return (acc0 + acc1) + (acc2 + acc3)

    own_even = ((iota((2, 16, 128), 0) + iota((2, 16, 128), 1)) & 1) == 0

    def half_sweep_0(colour, start, stop, lo=-4, hi=20):
        rows_even = even_row if hi - lo == 24 else own_even
        for i in range(start, stop, 2):
            vx[colour, i + 5:i + 7, lo + 8:hi + 8] = update_0(colour, i, lo, hi, rows_even)
    for copy in send_k:
        copy.wait_recv()
    couplings_0(0, -4, 20)
    couplings_0(1, -4, 20)
    for copy in send_v:
        copy.wait_recv()
    for colour in (0, 1):
        for i in range(-4, 20, 2):
            s0[colour, i + 4:i + 6] = s0[colour, i + 4:i + 6] * vx[colour, i + 5:i + 7, 4:28]

    half_sweep_0(0, -4, 20)
    half_sweep_0(1, -4, 20)
    half_sweep_0(0, -2, 18)
    half_sweep_0(1, -2, 18)
    def residual_0(i):
        total = None
        for colour in (0, 1):
            left = update_0(colour, i, 0, 16, own_even) - vx[colour, i + 5:i + 7, 8:24]
            left = d0[colour, i + 4:i + 6, 4:20] * left
            total = left if total is None else total + left
        return total

    for i in range(8):
        both = residual_0(2 * i)
        t0[i] = both[0] + both[1]
    rows = block_mean()
    for a in range(4):
        s1x[0, a + 4, 16:24], s1x[1, a + 4, 16:24] = merge(rows[2 * a], rows[2 * a + 1], odd_8)
    send_s1 = halo_copies(s1x, (4, 16), s1x, (4, 16), (4, 8), (3, 5), halo_sems.at[3], position)
    for copy in send_s1:
        copy.start()

    swap_k.wait_recv()
    mix(0, kg)
    for copy in spread_k:
        copy.start()
    vk[5:21, 8:24] = vx[1, 5:21, 8:24]
    send_vk = halo_copies(vk, (5, 8), vk, (5, 8), (16, 16), (4, 4), halo_sems.at[4], position)
    for copy in send_vk:
        copy.start()

    shape = (24, 128)
    col, lanes = iota(shape, 0) - 6, iota(shape, 1)
    w1 = 0.5 / 4.0
    wy_low = jnp.where((col == 0) & (gy == 0), 0.0, w1).astype(F32)
    wy_high = jnp.where((col == 7) & (gy == GY - 1), 0.0, w1).astype(F32)
    wx_low = jnp.where(gx == 0, 0.0, w1).astype(F32)
    wx_high = jnp.where(gx == GX - 1, 0.0, w1).astype(F32)
    wz_low = jnp.where(lanes == 0, 0.0, w1).astype(F32)
    wz_high = jnp.where(lanes == 127, 0.0, w1).astype(F32)

    def first_of_pair(size, origin):
        odd = (iota((size, 128), 0) + iota((size, 128), 1) + origin) & 1
        return odd == 0, odd == 1

    first_24, first_16, first_8 = first_of_pair(24, 0), first_of_pair(16, 0), first_of_pair(8, 0)
    for copy in send_k1:
        copy.wait_recv()
    for colour in (0, 1):
        for a in range(-3, 7):
            e, f = a + 4, a + 3
            other = k1[1 - colour, e, 10:34]
            first = first_24[colour]
            w_cross = w1
            if a in (0, 3):
                w_cross = jnp.where(first, wx_low if a == 0 else w1, wx_high if a == 3 else w1)
            parts, total, inverse = couple(
                k1[colour, e, 10:34], other, jnp.where(first, k1[1 - colour, e - 1, 10:34], k1[1 - colour, e + 1, 10:34]),
                k1[1 - colour, e, 9:33], k1[1 - colour, e, 11:35], other, (w1, w_cross, wy_low, wy_high, wz_low, wz_high), 1,
            )
            d1[colour, f] = total
            i1[colour, f] = inverse
            for n in range(6):
                c1[colour, n, f] = parts[n]

    def update_1(colour, a, lo, hi):
        e, f = a + 4, a + 3
        here, at = slice(lo + 6, hi + 6), slice(lo + 16, hi + 16)
        first = {24: first_24, 16: first_16, 8: first_8}[hi - lo][colour]
        return relax(
            s1[colour, f, here], [c1[colour, n, f, here] for n in range(6)], v1[1 - colour, e, at],
            jnp.where(first, v1[1 - colour, e - 1, at], v1[1 - colour, e + 1, at]),
            v1[1 - colour, e, lo + 15:hi + 15], v1[1 - colour, e, lo + 17:hi + 17], 1,
        )

    def half_sweep_1(colour, start, stop, lo, hi):
        for a in range(start, stop):
            v1[colour, a + 4, lo + 16:hi + 16] = update_1(colour, a, lo, hi)

    for copy in send_s1:
        copy.wait_recv()
    for colour in (0, 1):
        for a in range(-3, 7):
            s1[colour, a + 3] = i1[colour, a + 3] * s1x[colour, a + 4, 10:34]
    for a in range(-2, 6):
        v1[0, a + 4, 12:28] = s1[0, a + 3, 2:18]
    half_sweep_1(1, -2, 6, -4, 12)
    half_sweep_1(0, -1, 5, -4, 12)
    half_sweep_1(1, -1, 5, -4, 12)
    pairs = []
    for a in range(4):
        left = [d1[n, a + 3, 6:14] * (update_1(n, a, 0, 8) - v1[n, a + 4, 16:24]) for n in (0, 1)]
        pairs.append(left[0] + left[1])
    level_2_share(1, pairs)
    swap_s, spread_s, share_s = gather_copies(1, sg)
    swap_s.start()
    vk1[4:8, 16:24] = v1[1, 4:8, 16:24]
    send_vk1 = halo_copies(vk1, (4, 16), vk1, (4, 16), (4, 8), (3, 6), halo_sems.at[5], position)
    swap_s.wait_recv()
    mix(1, sg)
    for copy in spread_s:
        copy.start()
    for copy in send_vk1:
        copy.start()

    pass_on(0, share_k)
    lane = iota((64, 128), 1)
    place = lane & 63
    j_row = iota((64, 128), 0)
    low_64 = lane < 64
    first_64 = first_of_pair(64, 0)
    w2 = 0.5 / 16.0
    wy_low = jnp.where(j_row == 0, 0.0, w2).astype(F32)
    wy_high = jnp.where(j_row == 63, 0.0, w2).astype(F32)
    wz_low = jnp.where(place == 0, 0.0, w2).astype(F32)
    wz_high = jnp.where(place == 63, 0.0, w2).astype(F32)

    def cross_2(ref, colour, x, a, at, low, first):
        before, after = lax.rem(x + 3, 4), lax.rem(x + 1, 4)
        if a == 0:
            turned = roll(jnp.where(low, ref[colour, x, 1, at], ref[colour, before, 1, at]), 64)
            return jnp.where(first, turned, ref[colour, x, 1, at])
        turned = roll(jnp.where(low, ref[colour, after, 0, at], ref[colour, x, 0, at]), 64)
        return jnp.where(first, ref[colour, x, 0, at], turned)

    at = slice(8, 72)
    for colour in (0, 1):
        for x in range(4):
            for a in range(2):
                other = kg[1 - colour, x, a, at]
                w_cross = w2
                if (x, a) == (0, 0):
                    w_cross = jnp.where(first_64[colour] & low_64, 0.0, w2).astype(F32)
                if (x, a) == (3, 1):
                    w_cross = jnp.where(first_64[colour] | low_64, w2, 0.0).astype(F32)
                parts, total, inverse = couple(
                    kg[colour, x, a, at], other, cross_2(kg, 1 - colour, x, a, at, low_64, first_64[colour]),
                    kg[1 - colour, x, a, 7:71], kg[1 - colour, x, a, 9:73], other,
                    (w2, w_cross, wy_low, wy_high, wz_low, wz_high), 1,
                )
                d2[colour, x, a] = total
                i2[colour, x, a] = inverse
                for n in range(6):
                    c2[colour, n, x, a, at] = parts[n]
    even_place = (lane & 1) == 0
    lane3 = iota((32, 128), 1)
    place3 = (lane3 & 63) >> 1
    row3 = iota((32, 128), 0)
    low3 = lane3 < 64
    odd3 = ((row3 + place3) & 1) == 1
    first3 = (jnp.logical_not(odd3), odd3)

    def level_3_share(x, pairs):
        for a in range(2):
            t2[x, a] = pairs[a] + jnp.where(even_place, roll(pairs[a], -1), roll(pairs[a], 1))
        rows = [0.125 * (t2[x, a, pl.ds(0, 32, stride=2)] + t2[x, a, pl.ds(1, 32, stride=2)]) for a in range(2)]
        return merge(rows[0], rows[1], odd3)

    w3 = 0.5 / 64.0
    wy_low = jnp.where(row3 == 0, 0.0, w3).astype(F32)
    wy_high = jnp.where(row3 == 31, 0.0, w3).astype(F32)
    wz_low = jnp.where(place3 == 0, 0.0, w3).astype(F32)
    wz_high = jnp.where(place3 == 31, 0.0, w3).astype(F32)
    at3 = slice(8, 40)

    def cross_3(ref, colour, x, first):
        here = ref[colour, x, at3]
        before = jnp.where(low3, here, ref[colour, (x + 3) % 4, at3])
        after = jnp.where(low3, ref[colour, (x + 1) % 4, at3], here)
        return roll(jnp.where(first, before, after), 64)

    for x in range(4):
        k3[0, x, at3], k3[1, x, at3] = level_3_share(x, [kg[0, x, a, at] + kg[1, x, a, at] for a in range(2)])
    for colour in (0, 1):
        for x in range(4):
            other = k3[1 - colour, x, at3]
            w_cross = w3
            if x == 0:
                w_cross = jnp.where(first3[colour] & low3, 0.0, w3).astype(F32)
            if x == 3:
                w_cross = jnp.where(first3[colour] | low3, w3, 0.0).astype(F32)
            parts, _, inverse = couple(
                k3[colour, x, at3], other, cross_3(k3, 1 - colour, x, first3[colour]),
                k3[1 - colour, x, 7:39], k3[1 - colour, x, 9:41], other, (w3, w_cross, wy_low, wy_high, wz_low, wz_high), 2,
            )
            i3[colour, x] = inverse
            for n in range(6):
                c3[colour, n, x] = parts[n]
    pass_on(1, share_s)

    for colour in (0, 1):
        for x in range(4):
            for a in range(2):
                source = i2[colour, x, a] * sg[colour, x, a, at]
                s2[colour, x, a, at] = source
                if colour == 0:
                    v2[0, x, a, at] = source

    def update_2(colour, x, a, at, before, after, low, first):
        return relax(
            s2[colour, x, a, at], [c2[colour, n, x, a, at] for n in range(6)], v2[1 - colour, x, a, at],
            cross_2(v2, 1 - colour, x, a, at, low, first[colour]), v2[1 - colour, x, a, before], v2[1 - colour, x, a, after], 1,
        )

    def half_sweep_2(colour):
        for x in range(4):
            for a in range(2):
                v2[colour, x, a, at] = update_2(colour, x, a, at, slice(7, 71), slice(9, 73), low_64, first_64)

    half_sweep_2(1)
    half_sweep_2(0)
    half_sweep_2(1)
    for x in range(4):
        pairs = []
        for a in range(2):
            total = None
            for colour in (0, 1):
                left = update_2(colour, x, a, at, slice(7, 71), slice(9, 73), low_64, first_64) - v2[colour, x, a, at]
                left = d2[colour, x, a] * left
                total = left if total is None else total + left
            pairs.append(total)
        sources = level_3_share(x, pairs)
        for colour in (0, 1):
            s3[colour, x] = i3[colour, x] * sources[colour]

    def half_sweep_3(colour):
        for x in range(4):
            v3[colour, x, at3] = relax(
                s3[colour, x], [c3[colour, n, x] for n in range(6)], v3[1 - colour, x, at3],
                cross_3(v3, 1 - colour, x, first3[colour]), v3[1 - colour, x, 7:39], v3[1 - colour, x, 9:41], 2,
            )

    for x in range(4):
        v3[0, x, at3] = s3[0, x]
    half_sweep_3(1)
    for _ in range(COARSE_SWEEPS - 1):
        half_sweep_3(0)
        half_sweep_3(1)

    for x in range(4):
        red, black = v3[0, x, at3], v3[1, x, at3]
        for a, row in enumerate((jnp.where(odd3, black, red), jnp.where(odd3, red, black))):
            p2[x, a, pl.ds(8, 32, stride=2)] = row
            p2[x, a, pl.ds(9, 32, stride=2)] = row
    strip = gy // 2
    strip = pl.multiple_of(8 * (strip + 1 - (strip + 7) // 8 - (strip + 1) // 8), 8)
    at, before, after = pl.ds(strip, 24), pl.ds(strip - 1, 24), pl.ds(strip + 1, 24)
    xs = [lax.rem(chip_x + n, 4) for n in (3, 0, 1)]
    low_24 = iota((24, 128), 1) < 64
    for x in xs:
        for a in range(2):
            v2[1, x, a, at] = v2[1, x, a, at] + p2[x, a, at]
    for colour in (0, 1, 0, 1):
        news = [update_2(colour, x, a, at, before, after, low_24, first_24) for x in xs for a in range(2)]
        for n, new in enumerate(news):
            v2[colour, xs[n // 2], n % 2, at] = new

    spot = iota((10, 128), 1) >> 1
    odd_10 = (iota((10, 128), 0) + iota((10, 128), 1) + 1) & 1
    for d in range(-3, 7):
        row = 4 * core + d + 8
        x = lax.rem(chip_x + 3 + row // 8, 4)
        where = spot + 64 * (lax.rem(row, 8) // 4)
        cells = (x, d % 4 // 2, pl.ds(4 * gy + 5, 10))
        coarse = jnp.where(odd_10 == d % 2, v2[(0,) + cells], v2[(1,) + cells])
        coarse = jnp.take_along_axis(coarse, where, axis=1)
        p1[d + 3, pl.ds(0, 10, stride=2)] = coarse
        p1[d + 3, pl.ds(1, 10, stride=2)] = coarse
    for copy in send_vk1:
        copy.wait_recv()
    for a in range(-3, 7):
        v1[1, a + 4, 10:30] = vk1[a + 4, 10:30] + p1[a + 3]
    half_sweep_1(0, -3, 7, -6, 18)
    half_sweep_1(1, -2, 6, -4, 12)
    half_sweep_1(0, -2, 6, -4, 12)
    half_sweep_1(1, -1, 5, -4, 12)

    odd_12 = (iota((12, 128), 0) + iota((12, 128), 1)) & 1
    for i in range(-2, 10):
        a = i // 2
        row = jnp.where(odd_12 == i % 2, v1[0, a + 4, 14:26], v1[1, a + 4, 14:26])
        p0[i + 2, pl.ds(0, 12, stride=2)] = row
        p0[i + 2, pl.ds(1, 12, stride=2)] = row
    for copy in send_vk:
        copy.wait_recv()
    for i in range(-4, 20):
        vx[1, i + 5, 4:28] = vk[i + 5, 4:28] + p0[i // 2 + 2]
    half_sweep_0(0, -4, 20)
    half_sweep_0(1, -2, 18)
    half_sweep_0(0, -2, 18)
    half_sweep_0(1, 0, 16, 0, 16)
    for i in range(16):
        out[i, :, :128], out[i, :, 128:] = join(vx[0, i + 5, 8:24], vx[1, i + 5, 8:24], i & 1)
    for copy in send_k + send_v + send_k1 + send_s1 + send_vk + send_vk1 + [swap_k, swap_s] + share_k + share_s:
        copy.wait_send()
    for kind in (0, 1):
        for x in range(4):
            landed(kind, x, 0)


def v_cycle(image, conduct):
    def vmem(*shape):
        return pltpu.VMEM(shape, F32)

    frame0, frame1, frame2, frame3 = (26, 32, 128), (12, 40, 128), (4, 2, 80, 128), (2, 4, 48, 128)
    return pl.pallas_call(
        kernel,
        out_shape=jax.ShapeDtypeStruct((16, 16, 256), F32),
        in_specs=[pl.BlockSpec(memory_space=pltpu.HBM)] * 2,
        out_specs=pl.BlockSpec(memory_space=pltpu.VMEM),
        scratch_shapes=[
            vmem(16, 16, 256), vmem(16, 16, 256),
            vmem(2, *frame0), vmem(2, *frame0), vmem(2, 16, 16, 128), vmem(*frame0), vmem(2, 6, 24, 24, 128),
            vmem(2, 24, 24, 128), vmem(2, 24, 24, 128), vmem(8, 16, 128), vmem(12, 24, 128),
            vmem(2, *frame1), vmem(2, *frame1), vmem(2, *frame1), vmem(*frame1), vmem(2, 6, 10, 24, 128),
            vmem(2, 10, 24, 128), vmem(2, 10, 24, 128), vmem(2, 10, 24, 128), vmem(4, 8, 128), vmem(10, 20, 128),
            vmem(2, 2, 2, 4, 128), vmem(2, 2, 4, 128), vmem(2, 2, 4, 128),
            vmem(2, *frame2), vmem(2, *frame2), vmem(2, *frame2),
            vmem(2, 6, *frame2), vmem(2, *frame2), vmem(2, 4, 2, 64, 128), vmem(2, 4, 2, 64, 128), vmem(4, 2, 64, 128),
            vmem(*frame2),
            vmem(*frame3), vmem(*frame3), vmem(2, 6, 4, 32, 128), vmem(2, 4, 32, 128),
            vmem(2, 4, 32, 128), vmem(16, 2, 4, 128),
            pltpu.SemaphoreType.DMA((6, 2, 12)), pltpu.SemaphoreType.DMA((2, 9, 2)), pltpu.SemaphoreType.DMA((2,)),
        ],
        compiler_params=pltpu.CompilerParams(
            collective_id=0, has_side_effects=True, vmem_limit_bytes=48 * 2**20
        ),
        name="v_cycle",
    )(image, conduct)


def solution(mesh):
    return jax.shard_map(
        v_cycle,
        mesh=mesh,
        in_specs=(P("gx", "gy", None), P("gx", "gy", None)),
        out_specs=P("gx", "gy", None),
        check_vma=False,
    )
```

time: 56.5 us -> 44.8 us (0.79)
  Pallas kernels: 53.7 us -> 42 us
    pallas_call x1, Pallas kernels: 53.7 us -> 42 us  [v_cycle(): pl.pallas_call(kernel, out_shape=jax.ShapeDtypeStruct((16, 16, 256), F32)...]
where the time goes in v2:
time: 44.8 us; the launch traced here: 44.6 us
  Pallas kernels  42 us (94%)
  local copies, waits for them, and re-layouts  2.6 us (6%)
    pallas_call x1, Pallas kernels, v_cycle(): pl.pallas_call(kernel, out_shape=jax.ShapeDtypeStruct((16, 16, 256), F32)...  42 us
    unnamed x5, local copies, waits for them, and re-layouts  2.6 us

profile of v2, /device:TPU:1, one launch (start us, length us, event | category | flops | bytes accessed | tf_op | source)
XLA Modules:
  0.0 44.6 jit_solution(6012771158423303501)
XLA Ops:
  0.0 0.0 copy-start
  0.0 0.9 %copy-done = f32[16,16,256]{2,1,0:T(8,128)S(1)} copy-done((f32[16,16,256]{2,1,0:T(8,128)S(1)}, f32[16,16,256]{2,1,0:T(8,128)}, u32[]{:S(2)}) %copy-start) | copy-done | bytes 262168
  1.0 0.0 copy-start.1
  1.0 0.9 %copy-done.1 = f32[16,16,256]{2,1,0:T(8,128)S(1)} copy-done((f32[16,16,256]{2,1,0:T(8,128)S(1)}, f32[16,16,256]{2,1,0:T(8,128)}, u32[]{:S(2)}) %copy-start.1) | copy-done | bytes 262168
  1.9 42.0 %v_cycle.1 = f32[16,16,256]{2,1,0:T(8,128)S(1)} custom-call(f32[16,16,256]{2,1,0:T(8,128)S(1)} %copy-done, f32[16,16,256]{2,1,0:T(8,128)S(1)} %copy-done.1), custom_call_target="tpu_custom_call" | custom-call | tf_op jit(solution)/shard_map/v_cycle/pallas_call | solution.py:593
  43.9 0.7 %copy.4 = f32[16,16,256]{2,1,0:T(8,128)} copy(f32[16,16,256]{2,1,0:T(8,128)S(1)} %v_cycle.1) | data formatting | bytes 524288
Async XLA Ops:
  0.0 0.9 %copy-start = (f32[16,16,256]{2,1,0:T(8,128)S(1)}, f32[16,16,256]{2,1,0:T(8,128)}, u32[]{:S(2)}) copy-start(f32[16,16,256]{2,1,0:T(8,128)} %image.1) | copy-start | bytes 786436
  1.0 0.9 %copy-start.1 = (f32[16,16,256]{2,1,0:T(8,128)S(1)}, f32[16,16,256]{2,1,0:T(8,128)}, u32[]{:S(2)}) copy-start(f32[16,16,256]{2,1,0:T(8,128)} %conduct.1) | copy-start | bytes 786436

commit v3 on v2

v3 whole, which is shorter than its diff:
```python
import jax
import jax.numpy as jnp
from jax import lax
from jax.experimental import pallas as pl
from jax.experimental.pallas import tpu as pltpu
from jax.sharding import PartitionSpec as P

COARSE_SWEEPS = 8
MESH = pl.DeviceIdType.MESH
F32 = jnp.float32
GX, GY = 8, 16
DIRECTIONS = [(-1, -1), (-1, 1), (1, -1), (1, 1), (0, -1), (0, 1), (-1, 0), (1, 0)]
CHIPS = sorted(
    [(x, y, z) for x in range(4) for y in range(4) for z in range(4) if (x, y, z) != (0, 0, 0)],
    key=lambda d: -sum(min(c, 4 - c) for c in d),
)


def iota(shape, dim):
    return lax.broadcasted_iota(jnp.int32, shape, dim)


def roll(values, shift):
    return pltpu.roll(values, shift % 128, values.ndim - 1)


def halo_copies(src, src_origin, dst, origin, extent, widths, sems, position, corners=None):
    gx, gy = position
    lead = (slice(None),) * (len(dst.shape) - 3)

    def piece(step, size, here, there, start, stop):
        if step == 0:
            return slice(here, here + size), slice(there, there + size)
        if step > 0:
            return slice(here + size - stop, here + size - start), slice(there - stop, there - start)
        return slice(here + start, here + stop), slice(there + size + start, there + size + stop)

    copies, index = [], 0
    for dx, dy in DIRECTIONS:
        boxes = [((0, widths[0]), (0, widths[1]))]
        if dx and dy and corners is not None:
            boxes = [((start, stop), (0, width)) for start, stop, width in corners]
        group = []
        for box_x, box_y in boxes:
            src_x, dst_x = piece(dx, extent[0], src_origin[0], origin[0], *box_x)
            src_y, dst_y = piece(dy, extent[1], src_origin[1], origin[1], *box_y)
            group.append(
                pltpu.make_async_remote_copy(
                    src_ref=src.at[lead + (src_x, src_y)],
                    dst_ref=dst.at[lead + (dst_x, dst_y)],
                    send_sem=sems.at[0, index],
                    recv_sem=sems.at[1, index],
                    device_id=(lax.rem(gx + dx + GX, GX), lax.rem(gy + dy + GY, GY)),
                    device_id_type=MESH,
                )
            )
            index += 1
        copies.append((in_grid(gx + dx, gy + dy), in_grid(gx - dx, gy - dy), group))
    return copies


def in_grid(x, y):
    return (x >= 0) & (x < GX) & (y >= 0) & (y < GY)


def halo_start(copies):
    for sends, _, group in copies:

        @pl.when(sends)
        def _():
            for copy in group:
                copy.start()


def halo_wait(copies):
    for _, receives, group in copies:

        @pl.when(receives)
        def _():
            for copy in group:
                copy.wait_recv()


def halo_sent(copies):
    for sends, _, group in copies:

        @pl.when(sends)
        def _():
            for copy in group:
                copy.wait_send()


def couple(here, same, cross, low, high, other, weights, z_step):
    w, w_cross, w_low, w_high, w_below, w_above = weights
    parts = [
        (here + same) * w,
        (here + cross) * w_cross,
        (here + low) * w_low,
        (here + high) * w_high,
        (here + roll(other, z_step)) * w_below,
        (here + roll(other, -z_step)) * w_above,
    ]
    total = ((parts[0] + parts[1]) + (parts[2] + parts[3])) + ((parts[4] + parts[5]) + 1.0)
    inverse = 1.0 / total
    return [part * inverse for part in parts], total, inverse


def relax(source, couplings, same, cross, low, high, z_step):
    acc0 = source + couplings[0] * same
    acc1 = couplings[4] * roll(same, z_step) + couplings[5] * roll(same, -z_step)
    acc2 = couplings[2] * low + couplings[3] * high
    return (acc0 + acc2) + (acc1 + couplings[1] * cross)


def kernel(
    image, conduct, out,
    image_in, conduct_in, kx, vx, vs, vk, c0, s0, d0, t0, p0,
    k1, s1x, v1, vk1, c1, s1, i1, d1, t1, p1,
    q1, own2, kg, sg, v2, c2, s2, i2, d2, t2, p2,
    k3, v3, c3, s3, i3, dummy,
    halo_sems, gather_sems, tree_sems, in_sems,
):
    gx, gy = lax.axis_index("gx"), lax.axis_index("gy")
    chip_x, core = gx // 2, lax.rem(gx, 2)
    chip_z, chip_y = gy // 4, lax.rem(gy, 4)
    sibling = (chip_x * 2 + 1 - core, gy)
    chips = [
        (lax.rem(chip_x + x, 4) * 2 + core, lax.rem(chip_z + z, 4) * 4 + lax.rem(chip_y + y, 4))
        for x, y, z in CHIPS
    ]
    position = (gx, gy)
    barrier = pltpu.get_barrier_semaphore()
    greeted = chips + [
        (lax.rem(gx + dx + GX, GX), lax.rem(gy + dy + GY, GY)) for dx, dy in DIRECTIONS if dx
    ]
    fetch_k = pltpu.make_async_copy(conduct, conduct_in, in_sems.at[0])
    fetch_v = pltpu.make_async_copy(image, image_in, in_sems.at[1])
    fetch_k.start()
    fetch_v.start()
    for peer in greeted:
        pl.semaphore_signal(barrier, inc=1, device_id=peer, device_id_type=MESH)

    lane0 = iota((16, 128), 1)
    odd_row = iota((16, 128), 0) & 1
    low0 = lane0 < 64
    half_lane = (lane0 & 63) * 2

    def split(values, par):
        parity = odd_row ^ par
        first = half_lane + jnp.where(low0, parity, 1 - parity)
        second = half_lane + jnp.where(low0, 1 - parity, parity)
        left = jnp.take_along_axis(values[:, :128], first, axis=1)
        right = jnp.take_along_axis(values[:, 128:], second, axis=1)
        return jnp.where(low0, left, right), roll(jnp.where(low0, right, left), 64)

    def join(red, black, par):
        parity = odd_row ^ par
        turned = roll(black, 64)
        left, right = jnp.where(low0, red, turned), jnp.where(low0, turned, red)
        same = (lane0 & 1) == parity
        half = lane0 >> 1
        first = half + jnp.where(same, 0, 64)
        second = half + jnp.where(same, 64, 0)
        return jnp.take_along_axis(left, first, axis=1), jnp.take_along_axis(right, second, axis=1)
    nothing = jnp.zeros((2, 4, 4, 8, 128), F32)
    kg[:, :, :, 0:8], kg[:, :, :, 40:48] = nothing, nothing
    nothing = jnp.zeros((2, 20, 8, 128), F32)
    v2[:, :, 0:8], v2[:, :, 40:48] = nothing, nothing
    nothing = jnp.zeros((2, 2, 48, 128), F32)
    v2[:, 0:2], v2[:, 18:20] = nothing, nothing
    for ref in (k3, v3):
        nothing = jnp.zeros((2, 10, 8, 128), F32)
        ref[:, :, 0:8], ref[:, :, 24:32] = nothing, nothing
        nothing = jnp.zeros((2, 1, 32, 128), F32)
        ref[:, 0:1], ref[:, 9:10] = nothing, nothing

    def zero(ref, *at):
        at = (slice(None),) * (len(ref.shape) - 3) + at
        ref[at] = jnp.zeros(ref.at[at].shape, F32)

    for edge, rows0, rows1 in ((gx == 0, slice(0, 5), slice(0, 4)), (gx == GX - 1, slice(21, 26), slice(8, 12))):

        @pl.when(edge)
        def _():
            for ref in (kx, vx, vk):
                zero(ref, rows0)
            for ref in (k1, s1x, vk1):
                zero(ref, rows1)

    for edge, cols0, cols1 in ((gy == 0, slice(0, 8), slice(8, 16)), (gy == GY - 1, slice(24, 32), slice(24, 32))):

        @pl.when(edge)
        def _():
            for ref in (kx, vx, vk):
                zero(ref, slice(None), cols0)
            for ref in (k1, s1x, vk1):
                zero(ref, slice(None), cols1)

    fetch_k.wait()
    for i in range(16):
        kx[0, i + 5, 8:24], kx[1, i + 5, 8:24] = split(conduct_in[i], i & 1)
    pl.semaphore_wait(barrier, len(greeted))
    cone = [(0, 2, 4), (2, 4, 2)]
    send_k = halo_copies(kx, (5, 8), kx, (5, 8), (16, 16), (5, 5), halo_sems.at[0], position, cone)
    send_v = halo_copies(vs, (0, 0), vx, (5, 8), (16, 16), (5, 5), halo_sems.at[1], position, cone)
    halo_start(send_k)
    fetch_v.wait()
    for i in range(16):
        red, black = split(image_in[i], i & 1)
        vx[0, i + 5, 8:24], vx[1, i + 5, 8:24] = red, black
        vs[0, i], vs[1, i] = red, black
    halo_start(send_v)
    def block_mean():
        return [0.125 * (t0[i, pl.ds(0, 8, stride=2)] + t0[i, pl.ds(1, 8, stride=2)]) for i in range(8)]

    odd_8 = ((iota((8, 128), 0) + iota((8, 128), 1)) & 1) == 1
    odd_2 = ((iota((2, 128), 0) + iota((2, 128), 1)) & 1) == 1
    low_2 = iota((2, 128), 1) < 64
    even_lane = (iota((8, 128), 1) & 63) * 2

    def merge(first, second, odd):
        return jnp.where(odd, second, first), jnp.where(odd, first, second)

    def level_2_share(kind, pairs, whole):
        rows = []
        for i in range(4):
            t1[i] = jnp.take_along_axis(pairs[i], even_lane, axis=1) + jnp.take_along_axis(pairs[i], even_lane + 1, axis=1)
        for i in range(4):
            first = t1[i, pl.ds(0, 2, stride=2)] + t1[i, pl.ds(1, 2, stride=2)]
            second = t1[i, pl.ds(4, 2, stride=2)] + t1[i, pl.ds(5, 2, stride=2)]
            rows.append(0.125 * jnp.where(low_2, first, second))
        for a in range(2):
            cells = merge(rows[2 * a], rows[2 * a + 1], odd_2)
            for colour in (0, 1):
                own2[kind, colour, a] = cells[colour]
                whole[colour, chip_x, 2 * core + a, pl.ds(8 + 2 * gy, 2)] = cells[colour]

    def remote(src, dst, sems, device):
        return pltpu.make_async_remote_copy(
            src_ref=src, dst_ref=dst, send_sem=sems.at[0], recv_sem=sems.at[1], device_id=device, device_id_type=MESH
        )

    cores_rows = pl.ds(2 * core, 2)
    own_place = (slice(None), chip_x, cores_rows, pl.ds(8 + 2 * gy, 2))

    spread_s = [
        remote(own2.at[1], sg.at[own_place], gather_sems.at[x], chip) for chip, (x, _, _) in zip(chips, CHIPS)
    ]
    planes = [sg.at[:, lax.rem(chip_x + 4 - x, 4), cores_rows, 8:40] for x in range(4)]
    share_s = [remote(plane, plane, gather_sems.at[4 + x], sibling) for x, plane in enumerate(planes)]

    def landed(x, which):
        some = dummy.at[0:15] if x == 0 else dummy
        pltpu.make_async_copy(some, some, gather_sems.at[x, which]).wait()

    def chip_at(x, y, z):
        return (
            lax.rem(chip_x + x, 4) * 2 + core,
            lax.rem(chip_z + z, 4) * 4 + lax.rem(chip_y + y, 4),
        )

    column = kg.at[:, chip_x, cores_rows, pl.ds(8 + 8 * chip_z, 8)]
    sheet = kg.at[:, :, cores_rows, pl.ds(8 + 8 * chip_z, 8)]
    half = kg.at[:, :, cores_rows, 8:40]
    tree_y = [remote(own2.at[0], kg.at[own_place], tree_sems.at[n - 1], chip_at(0, n, 0)) for n in (2, 1, 3)]
    tree_x = [remote(column, column, tree_sems.at[n + 2], chip_at(n, 0, 0)) for n in (2, 1, 3)]
    tree_z = [remote(sheet, sheet, tree_sems.at[n + 5], chip_at(0, 0, n)) for n in (2, 1, 3)]
    tree_core = [remote(half, half, tree_sems.at[9], sibling)]

    for i in range(8):
        e = 2 * i + 5
        t0[i] = (kx[0, e, 8:24] + kx[1, e, 8:24]) + (kx[0, e + 1, 8:24] + kx[1, e + 1, 8:24])
    rows = block_mean()
    for a in range(4):
        k1[0, a + 4, 16:24], k1[1, a + 4, 16:24] = merge(rows[2 * a], rows[2 * a + 1], odd_8)
    level_2_share(0, [rows[2 * a] + rows[2 * a + 1] for a in range(4)], kg)
    send_k1 = halo_copies(k1, (4, 16), k1, (4, 16), (4, 8), (3, 6), halo_sems.at[2], position)
    halo_start(send_k1)
    for copy in tree_y:
        copy.start()

    shape = (2, 24, 128)
    sub, lanes = iota(shape, 1), iota(shape, 2)
    even_row = ((iota(shape, 0) + sub) & 1) == 0
    wy_low = jnp.where((sub == 4) & (gy == 0), 0.0, 0.5).astype(F32)
    wy_high = jnp.where((sub == 19) & (gy == GY - 1), 0.0, 0.5).astype(F32)
    wx_low = jnp.where(gx == 0, 0.0, 0.5).astype(F32)
    wx_high = jnp.where(gx == GX - 1, 0.0, 0.5).astype(F32)
    wz = [
        jnp.where(even_row, jnp.where(lanes == 0, 0.0, 0.5), jnp.where(lanes == 127, 0.0, 0.5)).astype(F32),
        jnp.where(even_row, jnp.where(lanes == 127, 0.0, 0.5), jnp.where(lanes == 0, 0.0, 0.5)).astype(F32),
    ]

    def beside(values, colour, rows_even):
        below, above = roll(values, 1), roll(values, -1)
        return jnp.where(rows_even, below, above) if colour == 0 else jnp.where(rows_even, above, below)

    row_index = iota((2, 1, 1), 0)

    def couplings_0(colour, start, stop):
        for i in range(start, stop, 2):
            e = i + 5
            here, other = kx[colour, e:e + 2, 4:28], kx[1 - colour, e:e + 2, 4:28]
            wx_l = jnp.where(row_index == 0, wx_low, 0.5) if i == 0 else 0.5
            wx_h = jnp.where(row_index == 1, wx_high, 0.5) if i == 14 else 0.5
            parts = [
                (here + kx[1 - colour, e - 1:e + 1, 4:28]) * wx_l,
                (here + kx[1 - colour, e + 1:e + 3, 4:28]) * wx_h,
                (here + kx[1 - colour, e:e + 2, 3:27]) * wy_low,
                (here + kx[1 - colour, e:e + 2, 5:29]) * wy_high,
                (here + other) * 0.5,
                (here + beside(other, colour, even_row)) * wz[colour],
            ]
            total = ((parts[0] + parts[1]) + (parts[2] + parts[3])) + ((parts[4] + parts[5]) + 1.0)
            inverse = 1.0 / total
            d0[colour, i + 4:i + 6] = total
            s0[colour, i + 4:i + 6] = inverse
            for n in range(6):
                c0[colour, n, i + 4:i + 6] = parts[n] * inverse

    def update_0(colour, i, lo, hi, rows_even):
        e, f = i + 5, i + 4
        a, b = lo + 8, hi + 8
        here = slice(lo + 4, hi + 4)
        other = vx[1 - colour, e:e + 2, a:b]
        acc0 = s0[colour, f:f + 2, here] + c0[colour, 0, f:f + 2, here] * vx[1 - colour, e - 1:e + 1, a:b]
        acc1 = c0[colour, 1, f:f + 2, here] * vx[1 - colour, e + 1:e + 3, a:b]
        acc1 += c0[colour, 2, f:f + 2, here] * vx[1 - colour, e:e + 2, a - 1:b - 1]
        acc2 = c0[colour, 3, f:f + 2, here] * vx[1 - colour, e:e + 2, a + 1:b + 1]
        acc2 += c0[colour, 4, f:f + 2, here] * other
        acc3 = c0[colour, 5, f:f + 2, here] * beside(other, colour, rows_even)
        return (acc0 + acc1) + (acc2 + acc3)

    own_even = ((iota((2, 16, 128), 0) + iota((2, 16, 128), 1)) & 1) == 0

    def half_sweep_0(colour, start, stop, lo=-4, hi=20):
        rows_even = even_row if hi - lo == 24 else own_even
        for i in range(start, stop, 2):
            vx[colour, i + 5:i + 7, lo + 8:hi + 8] = update_0(colour, i, lo, hi, rows_even)
    halo_wait(send_k)
    for copy in tree_y:
        copy.wait_recv()
    for copy in tree_x:
        copy.start()
    couplings_0(0, -4, 20)
    couplings_0(1, -4, 20)
    halo_wait(send_v)
    for colour in (0, 1):
        for i in range(-4, 20, 2):
            s0[colour, i + 4:i + 6] = s0[colour, i + 4:i + 6] * vx[colour, i + 5:i + 7, 4:28]

    half_sweep_0(0, -4, 20)
    half_sweep_0(1, -4, 20)
    half_sweep_0(0, -2, 18)
    half_sweep_0(1, -2, 18)
    def residual_0(i):
        total = None
        for colour in (0, 1):
            left = update_0(colour, i, 0, 16, own_even) - vx[colour, i + 5:i + 7, 8:24]
            left = d0[colour, i + 4:i + 6, 4:20] * left
            total = left if total is None else total + left
        return total

    for i in range(8):
        both = residual_0(2 * i)
        t0[i] = both[0] + both[1]
    rows = block_mean()
    for a in range(4):
        s1x[0, a + 4, 16:24], s1x[1, a + 4, 16:24] = merge(rows[2 * a], rows[2 * a + 1], odd_8)
    send_s1 = halo_copies(s1x, (4, 16), s1x, (4, 16), (4, 8), (3, 5), halo_sems.at[3], position)
    halo_start(send_s1)
    for copy in tree_x:
        copy.wait_recv()
    for copy in tree_z:
        copy.start()
    vk[5:21, 8:24] = vx[1, 5:21, 8:24]
    send_vk = halo_copies(vk, (5, 8), vk, (5, 8), (16, 16), (4, 4), halo_sems.at[4], position)
    halo_start(send_vk)

    shape = (24, 128)
    col, lanes = iota(shape, 0) - 6, iota(shape, 1)
    w1 = 0.5 / 4.0
    wy_low = jnp.where((col == 0) & (gy == 0), 0.0, w1).astype(F32)
    wy_high = jnp.where((col == 7) & (gy == GY - 1), 0.0, w1).astype(F32)
    wx_low = jnp.where(gx == 0, 0.0, w1).astype(F32)
    wx_high = jnp.where(gx == GX - 1, 0.0, w1).astype(F32)
    wz_low = jnp.where(lanes == 0, 0.0, w1).astype(F32)
    wz_high = jnp.where(lanes == 127, 0.0, w1).astype(F32)

    def first_of_pair(size, origin):
        odd = (iota((size, 128), 0) + iota((size, 128), 1) + origin) & 1
        return odd == 0, odd == 1

    first_24, first_16, first_8 = first_of_pair(24, 0), first_of_pair(16, 0), first_of_pair(8, 0)
    halo_wait(send_k1)
    for colour in (0, 1):
        for a in range(-3, 7):
            e, f = a + 4, a + 3
            other = k1[1 - colour, e, 10:34]
            first = first_24[colour]
            w_cross = w1
            if a in (0, 3):
                w_cross = jnp.where(first, wx_low if a == 0 else w1, wx_high if a == 3 else w1)
            parts, total, inverse = couple(
                k1[colour, e, 10:34], other, jnp.where(first, k1[1 - colour, e - 1, 10:34], k1[1 - colour, e + 1, 10:34]),
                k1[1 - colour, e, 9:33], k1[1 - colour, e, 11:35], other, (w1, w_cross, wy_low, wy_high, wz_low, wz_high), 1,
            )
            d1[colour, f] = total
            i1[colour, f] = inverse
            for n in range(6):
                c1[colour, n, f] = parts[n]

    def update_1(colour, a, lo, hi):
        e, f = a + 4, a + 3
        here, at = slice(lo + 6, hi + 6), slice(lo + 16, hi + 16)
        first = {24: first_24, 16: first_16, 8: first_8}[hi - lo][colour]
        return relax(
            s1[colour, f, here], [c1[colour, n, f, here] for n in range(6)], v1[1 - colour, e, at],
            jnp.where(first, v1[1 - colour, e - 1, at], v1[1 - colour, e + 1, at]),
            v1[1 - colour, e, lo + 15:hi + 15], v1[1 - colour, e, lo + 17:hi + 17], 1,
        )

    def half_sweep_1(colour, start, stop, lo, hi):
        for a in range(start, stop):
            v1[colour, a + 4, lo + 16:hi + 16] = update_1(colour, a, lo, hi)

    halo_wait(send_s1)
    for colour in (0, 1):
        for a in range(-3, 7):
            s1[colour, a + 3] = i1[colour, a + 3] * s1x[colour, a + 4, 10:34]
    for a in range(-2, 6):
        v1[0, a + 4, 12:28] = s1[0, a + 3, 2:18]
    half_sweep_1(1, -2, 6, -4, 12)
    half_sweep_1(0, -1, 5, -4, 12)
    half_sweep_1(1, -1, 5, -4, 12)
    pairs = []
    for a in range(4):
        left = [d1[n, a + 3, 6:14] * (update_1(n, a, 0, 8) - v1[n, a + 4, 16:24]) for n in (0, 1)]
        pairs.append(left[0] + left[1])
    level_2_share(1, pairs, sg)
    for copy in spread_s:
        copy.start()
    for copy in tree_z:
        copy.wait_recv()
    tree_core[0].start()
    vk1[4:8, 16:24] = v1[1, 4:8, 16:24]
    send_vk1 = halo_copies(vk1, (4, 16), vk1, (4, 16), (4, 8), (3, 6), halo_sems.at[5], position)
    halo_start(send_vk1)

    tree_core[0].wait_recv()
    def two_columns(size):
        return iota((size, 128), 1) < 64, (iota((size, 128), 0) & 1) == 1

    def beside_2(row_low, row_high, low, odd):
        turned = roll(jnp.where(low, row_high, row_low), 64)
        return jnp.where(odd, row_low, turned), jnp.where(odd, turned, row_high)

    lane = iota((32, 128), 1)
    place = lane & 63
    j_row = iota((32, 128), 0)
    low_32, odd_32 = two_columns(32)
    first_32 = first_of_pair(32, 0)
    w2 = 0.5 / 16.0
    wy_low = jnp.where((j_row == 0) & low_32, 0.0, w2).astype(F32)
    wy_high = jnp.where((j_row == 31) & (lane >= 64), 0.0, w2).astype(F32)
    wz_low = jnp.where(place == 0, 0.0, w2).astype(F32)
    wz_high = jnp.where(place == 63, 0.0, w2).astype(F32)

    def kg_rows(colour, a, at):
        return kg[colour, a // 4, a % 4, at]

    at = slice(8, 40)
    for colour in (0, 1):
        for a in range(16):
            other = kg_rows(1 - colour, a, at)
            before = kg_rows(1 - colour, max(a - 1, 0), at)
            after = kg_rows(1 - colour, min(a + 1, 15), at)
            w_cross = w2
            if a == 0:
                w_cross = jnp.where(first_32[colour], 0.0, w2).astype(F32)
            if a == 15:
                w_cross = jnp.where(first_32[colour], w2, 0.0).astype(F32)
            low, high = beside_2(
                kg_rows(1 - colour, a, slice(7, 39)), kg_rows(1 - colour, a, slice(9, 41)), low_32, odd_32
            )
            parts, total, inverse = couple(
                kg_rows(colour, a, at), other, jnp.where(first_32[colour], before, after), low, high, other,
                (w2, w_cross, wy_low, wy_high, wz_low, wz_high), 1,
            )
            d2[colour, a] = total
            i2[colour, a] = inverse
            for n in range(6):
                c2[colour, n, a] = parts[n]
    even_place = (lane & 1) == 0
    lane3 = iota((16, 128), 1)
    place3 = (lane3 & 63) >> 1
    row3 = iota((16, 128), 0)
    low3 = lane3 < 64
    odd3 = (((lane3 >> 6) + place3) & 1) == 1
    first3 = (jnp.logical_not(odd3), odd3)

    def level_3_share(p, pairs):
        for n in range(2):
            t2[2 * p + n] = pairs[n] + jnp.where(even_place, roll(pairs[n], -1), roll(pairs[n], 1))
        rows = [0.125 * (t2[2 * p + n, pl.ds(0, 16, stride=2)] + t2[2 * p + n, pl.ds(1, 16, stride=2)]) for n in range(2)]
        return merge(rows[0], rows[1], odd3)

    w3 = 0.5 / 64.0
    wy_low = jnp.where((row3 == 0) & low3, 0.0, w3).astype(F32)
    wy_high = jnp.where((row3 == 15) & (lane3 >= 64), 0.0, w3).astype(F32)
    wz_low = jnp.where(place3 == 0, 0.0, w3).astype(F32)
    wz_high = jnp.where(place3 == 31, 0.0, w3).astype(F32)
    at3 = slice(8, 24)

    def around_3(ref, colour, p, first):
        here = ref[colour, p + 1, at3]
        cross = jnp.where(first, ref[colour, p, at3], ref[colour, p + 2, at3])
        low = roll(jnp.where(low3, here, ref[colour, p + 1, 7:23]), 64)
        high = roll(jnp.where(low3, ref[colour, p + 1, 9:25], here), 64)
        return here, cross, low, high

    for p in range(8):
        pairs = [kg_rows(0, a, at) + kg_rows(1, a, at) for a in (2 * p, 2 * p + 1)]
        k3[0, p + 1, at3], k3[1, p + 1, at3] = level_3_share(p, pairs)
    for colour in (0, 1):
        for p in range(8):
            here, cross, low, high = around_3(k3, 1 - colour, p, first3[colour])
            w_cross = w3
            if p == 0:
                w_cross = jnp.where(first3[colour], 0.0, w3).astype(F32)
            if p == 7:
                w_cross = jnp.where(first3[colour], w3, 0.0).astype(F32)
            parts, _, inverse = couple(
                k3[colour, p + 1, at3], here, cross, low, high, here, (w3, w_cross, wy_low, wy_high, wz_low, wz_high), 2
            )
            i3[colour, p] = inverse
            for n in range(6):
                c3[colour, n, p] = parts[n]
    for x in (0, 1, 3, 2):
        landed(x, 1)
        share_s[x].start()
    for copy in share_s:
        copy.wait_recv()

    for colour in (0, 1):
        for a in range(16):
            source = i2[colour, a] * sg[colour, a // 4, a % 4, at]
            s2[colour, a] = source
            if colour == 0:
                v2[0, a + 2, at] = source

    def update_2(colour, a, rows, frame_rows, low, odd, first):
        before, here, after = frame_rows
        row_low, row_high = beside_2(v2[1 - colour, a + 2, before], v2[1 - colour, a + 2, after], low, odd)
        cross = jnp.where(first[colour], v2[1 - colour, a + 1, here], v2[1 - colour, a + 3, here])
        return relax(
            s2[colour, a, rows], [c2[colour, n, a, rows] for n in range(6)], v2[1 - colour, a + 2, here],
            cross, row_low, row_high, 1,
        )

    whole_2 = (slice(0, 32), (slice(7, 39), at, slice(9, 41)), low_32, odd_32, first_32)

    def half_sweep_2(colour):
        for a in range(16):
            v2[colour, a + 2, at] = update_2(colour, a, *whole_2)

    half_sweep_2(1)
    half_sweep_2(0)
    half_sweep_2(1)
    for p in range(8):
        pairs = []
        for a in (2 * p, 2 * p + 1):
            left = [d2[n, a] * (update_2(n, a, *whole_2) - v2[n, a + 2, at]) for n in (0, 1)]
            pairs.append(left[0] + left[1])
        sources = level_3_share(p, pairs)
        for colour in (0, 1):
            s3[colour, p] = i3[colour, p] * sources[colour]

    def half_sweep_3(colour):
        for p in range(8):
            here, cross, low, high = around_3(v3, 1 - colour, p, first3[colour])
            v3[colour, p + 1, at3] = relax(
                s3[colour, p], [c3[colour, n, p] for n in range(6)], here, cross, low, high, 2
            )

    for p in range(8):
        v3[0, p + 1, at3] = s3[0, p]
    half_sweep_3(1)
    for _ in range(COARSE_SWEEPS - 1):
        half_sweep_3(0)
        half_sweep_3(1)

    for p in range(8):
        red, black = v3[0, p + 1, at3], v3[1, p + 1, at3]
        for n, row in enumerate((jnp.where(odd3, black, red), jnp.where(odd3, red, black))):
            p2[2 * p + n, pl.ds(0, 16, stride=2)] = row
            p2[2 * p + n, pl.ds(1, 16, stride=2)] = row

    def within(value, top, span):
        value = value * ((value + span) // span)
        value = top - value
        return top - value * ((value + span) // span)

    a0 = 2 * within(gx - 2, 3, 8)
    r0 = 2 * within(gy - 2, 8, 16)
    strip = pl.ds(r0, 16)
    part_2 = (strip, (pl.ds(r0 + 7, 16), pl.ds(r0 + 8, 16), pl.ds(r0 + 9, 16)), *two_columns(16), first_16)
    for n in range(10):
        v2[1, a0 + n + 2, pl.ds(r0 + 8, 16)] = v2[1, a0 + n + 2, pl.ds(r0 + 8, 16)] + p2[a0 + n, strip]
    for colour in (0, 1, 0, 1):
        news = [update_2(colour, a0 + n, *part_2) for n in range(10)]
        for n, new in enumerate(news):
            v2[colour, a0 + n + 2, pl.ds(r0 + 8, 16)] = new

    spot = iota((8, 128), 1) >> 1
    for d in range(-3, 7):
        cells = (2 * gx + d // 2 + 2, pl.ds(2 * gy + 6, 8))
        coarse = jnp.where(odd_8 == (d % 2 == 1), v2[(0,) + cells], v2[(1,) + cells])
        q1[d + 3, 0] = jnp.take_along_axis(coarse, spot, axis=1)
        q1[d + 3, 1] = jnp.take_along_axis(coarse, spot + 64, axis=1)
    for d in range(10):
        for n in range(2):
            for m in range(2):
                column = q1[d, n, pl.ds(m, 4, stride=2)]
                p1[d, pl.ds(4 * n + 2 * m, 4, stride=8)] = column
                p1[d, pl.ds(4 * n + 2 * m + 1, 4, stride=8)] = column
    halo_wait(send_vk1)
    for a in range(-3, 7):
        v1[1, a + 4, 10:30] = vk1[a + 4, 10:30] + p1[a + 3, 2:22]
    half_sweep_1(0, -3, 7, -6, 18)
    half_sweep_1(1, -2, 6, -4, 12)
    half_sweep_1(0, -2, 6, -4, 12)
    half_sweep_1(1, -1, 5, -4, 12)

    odd_12 = (iota((12, 128), 0) + iota((12, 128), 1)) & 1
    for i in range(-2, 10):
        a = i // 2
        row = jnp.where(odd_12 == i % 2, v1[0, a + 4, 14:26], v1[1, a + 4, 14:26])
        p0[i + 2, pl.ds(0, 12, stride=2)] = row
        p0[i + 2, pl.ds(1, 12, stride=2)] = row
    halo_wait(send_vk)
    for i in range(-4, 20):
        vx[1, i + 5, 4:28] = vk[i + 5, 4:28] + p0[i // 2 + 2]
    half_sweep_0(0, -4, 20)
    half_sweep_0(1, -2, 18)
    half_sweep_0(0, -2, 18)
    half_sweep_0(1, 0, 16, 0, 16)
    for i in range(16):
        out[i, :, :128], out[i, :, 128:] = join(vx[0, i + 5, 8:24], vx[1, i + 5, 8:24], i & 1)
    for copies in (send_k, send_v, send_k1, send_s1, send_vk, send_vk1):
        halo_sent(copies)
    for copy in tree_y + tree_x + tree_z + tree_core + share_s:
        copy.wait_send()
    for x in range(4):
        landed(x, 0)


def v_cycle(image, conduct):
    def vmem(*shape):
        return pltpu.VMEM(shape, F32)

    frame0, frame1, gathered = (26, 32, 128), (12, 40, 128), (2, 4, 4, 48, 128)
    return pl.pallas_call(
        kernel,
        out_shape=jax.ShapeDtypeStruct((16, 16, 256), F32),
        in_specs=[pl.BlockSpec(memory_space=pltpu.HBM)] * 2,
        out_specs=pl.BlockSpec(memory_space=pltpu.VMEM),
        scratch_shapes=[
            vmem(16, 16, 256), vmem(16, 16, 256),
            vmem(2, *frame0), vmem(2, *frame0), vmem(2, 16, 16, 128), vmem(*frame0), vmem(2, 6, 24, 24, 128),
            vmem(2, 24, 24, 128), vmem(2, 24, 24, 128), vmem(8, 16, 128), vmem(12, 24, 128),
            vmem(2, *frame1), vmem(2, *frame1), vmem(2, *frame1), vmem(*frame1), vmem(2, 6, 10, 24, 128),
            vmem(2, 10, 24, 128), vmem(2, 10, 24, 128), vmem(2, 10, 24, 128), vmem(4, 8, 128), vmem(10, 32, 128),
            vmem(10, 2, 8, 128), vmem(2, 2, 2, 2, 128), vmem(*gathered), vmem(*gathered), vmem(2, 20, 48, 128),
            vmem(2, 6, 16, 32, 128), vmem(2, 16, 32, 128), vmem(2, 16, 32, 128), vmem(2, 16, 32, 128), vmem(16, 32, 128),
            vmem(16, 32, 128),
            vmem(2, 10, 32, 128), vmem(2, 10, 32, 128), vmem(2, 6, 8, 16, 128), vmem(2, 8, 16, 128),
            vmem(2, 8, 16, 128), vmem(16, 8, 128),
            pltpu.SemaphoreType.DMA((6, 2, 12)), pltpu.SemaphoreType.DMA((8, 2)), pltpu.SemaphoreType.DMA((10, 2)),
            pltpu.SemaphoreType.DMA((2,)),
        ],
        compiler_params=pltpu.CompilerParams(
            collective_id=0, has_side_effects=True, vmem_limit_bytes=48 * 2**20
        ),
        name="v_cycle",
    )(image, conduct)


def solution(mesh):
    return jax.shard_map(
        v_cycle,
        mesh=mesh,
        in_specs=(P("gx", "gy", None), P("gx", "gy", None)),
        out_specs=P("gx", "gy", None),
        check_vma=False,
    )
```

time: 44.8 us -> 41.2 us (0.920)
  Pallas kernels: 42 us -> 38.4 us
    pallas_call x1, Pallas kernels: 42 us -> 38.4 us  [v_cycle(): pl.pallas_call(kernel, out_shape=jax.ShapeDtypeStruct((16, 16, 256), F32)...]
where the time goes in v3:
time: 41.2 us; the launch traced here: 41 us
  Pallas kernels  38.4 us (93%)
  local copies, waits for them, and re-layouts  2.6 us (6%)
    pallas_call x1, Pallas kernels, v_cycle(): pl.pallas_call(kernel, out_shape=jax.ShapeDtypeStruct((16, 16, 256), F32)...  38.4 us
    unnamed x5, local copies, waits for them, and re-layouts  2.6 us

profile of v3, /device:TPU:1, one launch (start us, length us, event | category | flops | bytes accessed | tf_op | source)
XLA Modules:
  0.0 41.0 jit_solution(9774106068181924141)
XLA Ops:
  0.0 0.0 copy-start
  0.0 0.9 %copy-done = f32[16,16,256]{2,1,0:T(8,128)S(1)} copy-done((f32[16,16,256]{2,1,0:T(8,128)S(1)}, f32[16,16,256]{2,1,0:T(8,128)}, u32[]{:S(2)}) %copy-start) | copy-done | bytes 262168
  1.0 0.0 copy-start.1
  1.0 0.9 %copy-done.1 = f32[16,16,256]{2,1,0:T(8,128)S(1)} copy-done((f32[16,16,256]{2,1,0:T(8,128)S(1)}, f32[16,16,256]{2,1,0:T(8,128)}, u32[]{:S(2)}) %copy-start.1) | copy-done | bytes 262168
  1.9 38.4 %v_cycle.1 = f32[16,16,256]{2,1,0:T(8,128)S(1)} custom-call(f32[16,16,256]{2,1,0:T(8,128)S(1)} %copy-done, f32[16,16,256]{2,1,0:T(8,128)S(1)} %copy-done.1), custom_call_target="tpu_custom_call" | custom-call | tf_op jit(solution)/shard_map/v_cycle/pallas_call | solution.py:663
  40.3 0.7 %copy.4 = f32[16,16,256]{2,1,0:T(8,128)} copy(f32[16,16,256]{2,1,0:T(8,128)S(1)} %v_cycle.1) | data formatting | bytes 524288
Async XLA Ops:
  0.0 0.9 %copy-start = (f32[16,16,256]{2,1,0:T(8,128)S(1)}, f32[16,16,256]{2,1,0:T(8,128)}, u32[]{:S(2)}) copy-start(f32[16,16,256]{2,1,0:T(8,128)} %image.1) | copy-start | bytes 786436
  1.0 0.9 %copy-start.1 = (f32[16,16,256]{2,1,0:T(8,128)S(1)}, f32[16,16,256]{2,1,0:T(8,128)}, u32[]{:S(2)}) copy-start(f32[16,16,256]{2,1,0:T(8,128)} %conduct.1) | copy-start | bytes 786436

commit v4 on v3

--- a/solution.py
+++ b/solution.py
@@ -118,7 +118,7 @@
     k1, s1x, v1, vk1, c1, s1, i1, d1, t1, p1,
     q1, own2, kg, sg, v2, c2, s2, i2, d2, t2, p2,
     k3, v3, c3, s3, i3, dummy,
-    halo_sems, gather_sems, tree_sems, in_sems,
+    halo_sems, gather_sems, tree_sems, in_sems, known_sems,
 ):
     gx, gy = lax.axis_index("gx"), lax.axis_index("gy")
     chip_x, core = gx // 2, lax.rem(gx, 2)
@@ -130,15 +130,24 @@
     ]
     position = (gx, gy)
     barrier = pltpu.get_barrier_semaphore()
-    greeted = chips + [
-        (lax.rem(gx + dx + GX, GX), lax.rem(gy + dy + GY, GY)) for dx, dy in DIRECTIONS if dx
-    ]
+
+    def ring(step):
+        offsets = sorted({((step * x) % GX, (step * y) % GY) for x, y in DIRECTIONS})
+        return [(lax.rem(gx + x, GX), lax.rem(gy + y, GY)) for x, y in offsets]
+
+    def tell(n):
+        for peer in ring(1 << n):
+            pl.semaphore_signal(known_sems.at[n], inc=1, device_id=peer, device_id_type=MESH)
+
+    def hear(n):
+        pl.semaphore_wait(known_sems.at[n], len(ring(1 << n)))
+
+    for peer in ring(1):
+        pl.semaphore_signal(barrier, inc=1, device_id=peer, device_id_type=MESH)
     fetch_k = pltpu.make_async_copy(conduct, conduct_in, in_sems.at[0])
     fetch_v = pltpu.make_async_copy(image, image_in, in_sems.at[1])
     fetch_k.start()
     fetch_v.start()
-    for peer in greeted:
-        pl.semaphore_signal(barrier, inc=1, device_id=peer, device_id_type=MESH)
 
     lane0 = iota((16, 128), 1)
     odd_row = iota((16, 128), 0) & 1
@@ -199,11 +208,12 @@
     fetch_k.wait()
     for i in range(16):
         kx[0, i + 5, 8:24], kx[1, i + 5, 8:24] = split(conduct_in[i], i & 1)
-    pl.semaphore_wait(barrier, len(greeted))
+    pl.semaphore_wait(barrier, len(ring(1)))
     cone = [(0, 2, 4), (2, 4, 2)]
     send_k = halo_copies(kx, (5, 8), kx, (5, 8), (16, 16), (5, 5), halo_sems.at[0], position, cone)
     send_v = halo_copies(vs, (0, 0), vx, (5, 8), (16, 16), (5, 5), halo_sems.at[1], position, cone)
     halo_start(send_k)
+    tell(0)
     fetch_v.wait()
     for i in range(16):
         red, black = split(image_in[i], i & 1)
@@ -259,13 +269,14 @@
             lax.rem(chip_z + z, 4) * 4 + lax.rem(chip_y + y, 4),
         )
 
-    column = kg.at[:, chip_x, cores_rows, pl.ds(8 + 8 * chip_z, 8)]
     sheet = kg.at[:, :, cores_rows, pl.ds(8 + 8 * chip_z, 8)]
     half = kg.at[:, :, cores_rows, 8:40]
-    tree_y = [remote(own2.at[0], kg.at[own_place], tree_sems.at[n - 1], chip_at(0, n, 0)) for n in (2, 1, 3)]
-    tree_x = [remote(column, column, tree_sems.at[n + 2], chip_at(n, 0, 0)) for n in (2, 1, 3)]
-    tree_z = [remote(sheet, sheet, tree_sems.at[n + 5], chip_at(0, 0, n)) for n in (2, 1, 3)]
-    tree_core = [remote(half, half, tree_sems.at[9], sibling)]
+    tree_xy = [
+        remote(own2.at[0], kg.at[own_place], tree_sems.at[n], chip_at(x, y, 0))
+        for n, (x, y) in enumerate((x, y) for x in range(4) for y in range(4) if x or y)
+    ]
+    tree_z = [remote(sheet, sheet, tree_sems.at[n + 14], chip_at(0, 0, n)) for n in (2, 1, 3)]
+    tree_core = [remote(half, half, tree_sems.at[18], sibling)]
 
     for i in range(8):
         e = 2 * i + 5
@@ -276,8 +287,6 @@
     level_2_share(0, [rows[2 * a] + rows[2 * a + 1] for a in range(4)], kg)
     send_k1 = halo_copies(k1, (4, 16), k1, (4, 16), (4, 8), (3, 6), halo_sems.at[2], position)
     halo_start(send_k1)
-    for copy in tree_y:
-        copy.start()
 
     shape = (2, 24, 128)
     sub, lanes = iota(shape, 1), iota(shape, 2)
@@ -337,13 +346,15 @@
         rows_even = even_row if hi - lo == 24 else own_even
         for i in range(start, stop, 2):
             vx[colour, i + 5:i + 7, lo + 8:hi + 8] = update_0(colour, i, lo, hi, rows_even)
+    hear(0)
+    tell(1)
     halo_wait(send_k)
-    for copy in tree_y:
-        copy.wait_recv()
-    for copy in tree_x:
-        copy.start()
     couplings_0(0, -4, 20)
     couplings_0(1, -4, 20)
+    hear(1)
+    tell(2)
+    for copy in tree_xy:
+        copy.start()
     halo_wait(send_v)
     for colour in (0, 1):
         for i in range(-4, 20, 2):
@@ -369,10 +380,7 @@
         s1x[0, a + 4, 16:24], s1x[1, a + 4, 16:24] = merge(rows[2 * a], rows[2 * a + 1], odd_8)
     send_s1 = halo_copies(s1x, (4, 16), s1x, (4, 16), (4, 8), (3, 5), halo_sems.at[3], position)
     halo_start(send_s1)
-    for copy in tree_x:
-        copy.wait_recv()
-    for copy in tree_z:
-        copy.start()
+
     vk[5:21, 8:24] = vx[1, 5:21, 8:24]
     send_vk = halo_copies(vk, (5, 8), vk, (5, 8), (16, 16), (4, 4), halo_sems.at[4], position)
     halo_start(send_vk)
@@ -423,6 +431,11 @@
     def half_sweep_1(colour, start, stop, lo, hi):
         for a in range(start, stop):
             v1[colour, a + 4, lo + 16:hi + 16] = update_1(colour, a, lo, hi)
+    hear(2)
+    for copy in tree_xy:
+        copy.wait_recv()
+    for copy in tree_z:
+        copy.start()
 
     halo_wait(send_s1)
     for colour in (0, 1):
@@ -491,8 +504,8 @@
             i2[colour, a] = inverse
             for n in range(6):
                 c2[colour, n, a] = parts[n]
-    even_place = (lane & 1) == 0
     lane3 = iota((16, 128), 1)
+    even_place = (lane3 & 1) == 0
     place3 = (lane3 & 63) >> 1
     row3 = iota((16, 128), 0)
     low3 = lane3 < 64
@@ -500,9 +513,12 @@
     first3 = (jnp.logical_not(odd3), odd3)
 
     def level_3_share(p, pairs):
+        rows = []
         for n in range(2):
-            t2[2 * p + n] = pairs[n] + jnp.where(even_place, roll(pairs[n], -1), roll(pairs[n], 1))
-        rows = [0.125 * (t2[2 * p + n, pl.ds(0, 16, stride=2)] + t2[2 * p + n, pl.ds(1, 16, stride=2)]) for n in range(2)]
+            t2[2 * p + n] = pairs[n]
+        for n in range(2):
+            row = t2[2 * p + n, pl.ds(0, 16, stride=2)] + t2[2 * p + n, pl.ds(1, 16, stride=2)]
+            rows.append(0.125 * (row + jnp.where(even_place, roll(row, -1), roll(row, 1))))
         return merge(rows[0], rows[1], odd3)
 
     w3 = 0.5 / 64.0
@@ -649,7 +665,7 @@
         out[i, :, :128], out[i, :, 128:] = join(vx[0, i + 5, 8:24], vx[1, i + 5, 8:24], i & 1)
     for copies in (send_k, send_v, send_k1, send_s1, send_vk, send_vk1):
         halo_sent(copies)
-    for copy in tree_y + tree_x + tree_z + tree_core + share_s:
+    for copy in tree_xy + tree_z + tree_core + share_s:
         copy.wait_send()
     for x in range(4):
         landed(x, 0)
@@ -676,8 +692,8 @@
             vmem(16, 32, 128),
             vmem(2, 10, 32, 128), vmem(2, 10, 32, 128), vmem(2, 6, 8, 16, 128), vmem(2, 8, 16, 128),
             vmem(2, 8, 16, 128), vmem(16, 8, 128),
-            pltpu.SemaphoreType.DMA((6, 2, 12)), pltpu.SemaphoreType.DMA((8, 2)), pltpu.SemaphoreType.DMA((10, 2)),
-            pltpu.SemaphoreType.DMA((2,)),
+            pltpu.SemaphoreType.DMA((6, 2, 12)), pltpu.SemaphoreType.DMA((8, 2)), pltpu.SemaphoreType.DMA((19, 2)),
+            pltpu.SemaphoreType.DMA((2,)), pltpu.SemaphoreType.REGULAR((3,)),
         ],
         compiler_params=pltpu.CompilerParams(
             collective_id=0, has_side_effects=True, vmem_limit_bytes=48 * 2**20

time: 41.2 us -> 39.9 us (0.968)
  Pallas kernels: 38.4 us -> 37 us
    pallas_call x1, Pallas kernels: 38.4 us -> 37 us  [v_cycle(): pl.pallas_call(kernel, out_shape=jax.ShapeDtypeStruct((16, 16, 256), F32)...]
where the time goes in v4:
time: 39.9 us; the launch traced here: 39.6 us
  Pallas kernels  37 us (93%)
  local copies, waits for them, and re-layouts  2.6 us (7%)
    pallas_call x1, Pallas kernels, v_cycle(): pl.pallas_call(kernel, out_shape=jax.ShapeDtypeStruct((16, 16, 256), F32)...  37 us
    unnamed x5, local copies, waits for them, and re-layouts  2.6 us

profile of v4, /device:TPU:1, one launch (start us, length us, event | category | flops | bytes accessed | tf_op | source)
XLA Modules:
  0.0 39.6 jit_solution(14335781510782883184)
XLA Ops:
  0.0 0.0 copy-start
  0.0 0.9 %copy-done = f32[16,16,256]{2,1,0:T(8,128)S(1)} copy-done((f32[16,16,256]{2,1,0:T(8,128)S(1)}, f32[16,16,256]{2,1,0:T(8,128)}, u32[]{:S(2)}) %copy-start) | copy-done | bytes 262168
  1.0 0.0 copy-start.1
  1.0 0.9 %copy-done.1 = f32[16,16,256]{2,1,0:T(8,128)S(1)} copy-done((f32[16,16,256]{2,1,0:T(8,128)S(1)}, f32[16,16,256]{2,1,0:T(8,128)}, u32[]{:S(2)}) %copy-start.1) | copy-done | bytes 262168
  1.9 37.0 %v_cycle.1 = f32[16,16,256]{2,1,0:T(8,128)S(1)} custom-call(f32[16,16,256]{2,1,0:T(8,128)S(1)} %copy-done, f32[16,16,256]{2,1,0:T(8,128)S(1)} %copy-done.1), custom_call_target="tpu_custom_call" | custom-call | tf_op jit(solution)/shard_map/v_cycle/pallas_call | solution.py:679
  38.9 0.7 %copy.4 = f32[16,16,256]{2,1,0:T(8,128)} copy(f32[16,16,256]{2,1,0:T(8,128)S(1)} %v_cycle.1) | data formatting | bytes 524288
Async XLA Ops:
  0.0 0.9 %copy-start = (f32[16,16,256]{2,1,0:T(8,128)S(1)}, f32[16,16,256]{2,1,0:T(8,128)}, u32[]{:S(2)}) copy-start(f32[16,16,256]{2,1,0:T(8,128)} %image.1) | copy-start | bytes 786436
  1.0 0.9 %copy-start.1 = (f32[16,16,256]{2,1,0:T(8,128)S(1)}, f32[16,16,256]{2,1,0:T(8,128)}, u32[]{:S(2)}) copy-start(f32[16,16,256]{2,1,0:T(8,128)} %conduct.1) | copy-start | bytes 786436

commit v5 on v4

--- a/solution.py
+++ b/solution.py
@@ -1,3 +1,5 @@
+import math
+
 import jax
 import jax.numpy as jnp
 from jax import lax
@@ -16,6 +18,10 @@
 )
 
 
+def nearness(offset):
+    return max(min(offset[0], GX - offset[0]), min(offset[1], GY - offset[1]))
+
+
 def iota(shape, dim):
     return lax.broadcasted_iota(jnp.int32, shape, dim)
 
@@ -35,7 +41,7 @@
             return slice(here + size - stop, here + size - start), slice(there - stop, there - start)
         return slice(here + start, here + stop), slice(there + size + start, there + size + stop)
 
-    copies, index = [], 0
+    copies = []
     for dx, dy in DIRECTIONS:
         boxes = [((0, widths[0]), (0, widths[1]))]
         if dx and dy and corners is not None:
@@ -48,14 +54,13 @@
                 pltpu.make_async_remote_copy(
                     src_ref=src.at[lead + (src_x, src_y)],
                     dst_ref=dst.at[lead + (dst_x, dst_y)],
-                    send_sem=sems.at[0, index],
-                    recv_sem=sems.at[1, index],
+                    send_sem=sems[0],
+                    recv_sem=sems[1],
                     device_id=(lax.rem(gx + dx + GX, GX), lax.rem(gy + dy + GY, GY)),
                     device_id_type=MESH,
                 )
             )
-            index += 1
-        copies.append((in_grid(gx + dx, gy + dy), in_grid(gx - dx, gy - dy), group))
+        copies.append((in_grid(gx + dx, gy + dy), group))
     return copies
 
 
@@ -64,7 +69,7 @@
 
 
 def halo_start(copies):
-    for sends, _, group in copies:
+    for sends, group in copies:
 
         @pl.when(sends)
         def _():
@@ -72,22 +77,29 @@
                 copy.start()
 
 
-def halo_wait(copies):
-    for _, receives, group in copies:
-
-        @pl.when(receives)
-        def _():
-            for copy in group:
-                copy.wait_recv()
-
-
-def halo_sent(copies):
-    for sends, _, group in copies:
-
-        @pl.when(sends)
-        def _():
-            for copy in group:
-                copy.wait_send()
+def rows_of(group):
+    return sum(math.prod(copy.src_ref.shape[:-1]) for copy in group)
+
+
+def wait_rows(rows, sem, room):
+    pltpu.make_async_copy(room.at[0:rows], room.at[0:rows], sem).wait()
+
+
+def halo_wait(exchanges, position, sem, room, more=0):
+    edge_x = (position[0] == 0) | (position[0] == GX - 1)
+    edge_y = (position[1] == 0) | (position[1] == GY - 1)
+    rows = {direction: 0 for direction in DIRECTIONS}
+    for copies in exchanges:
+        for direction, (_, group) in zip(DIRECTIONS, copies):
+            rows[direction] += rows_of(group)
+    for at_x in (False, True):
+        for at_y in (False, True):
+            lost = [(dx, dy) for dx, dy in DIRECTIONS if (at_x and dx == 1) or (at_y and dy == 1)]
+            total = more + sum(rows.values()) - sum(rows[direction] for direction in lost)
+
+            @pl.when((edge_x == at_x) & (edge_y == at_y))
+            def _():
+                wait_rows(total, sem, room)
 
 
 def couple(here, same, cross, low, high, other, weights, z_step):
@@ -118,7 +130,7 @@
     k1, s1x, v1, vk1, c1, s1, i1, d1, t1, p1,
     q1, own2, kg, sg, v2, c2, s2, i2, d2, t2, p2,
     k3, v3, c3, s3, i3, dummy,
-    halo_sems, gather_sems, tree_sems, in_sems, known_sems,
+    sent, arrived, in_sems, known_sems,
 ):
     gx, gy = lax.axis_index("gx"), lax.axis_index("gy")
     chip_x, core = gx // 2, lax.rem(gx, 2)
@@ -129,25 +141,28 @@
         for x, y, z in CHIPS
     ]
     position = (gx, gy)
+
     barrier = pltpu.get_barrier_semaphore()
 
-    def ring(step):
-        offsets = sorted({((step * x) % GX, (step * y) % GY) for x, y in DIRECTIONS})
-        return [(lax.rem(gx + x, GX), lax.rem(gy + y, GY)) for x, y in offsets]
-
-    def tell(n):
-        for peer in ring(1 << n):
-            pl.semaphore_signal(known_sems.at[n], inc=1, device_id=peer, device_id_type=MESH)
-
-    def hear(n):
-        pl.semaphore_wait(known_sems.at[n], len(ring(1 << n)))
-
-    for peer in ring(1):
-        pl.semaphore_signal(barrier, inc=1, device_id=peer, device_id_type=MESH)
     fetch_k = pltpu.make_async_copy(conduct, conduct_in, in_sems.at[0])
     fetch_v = pltpu.make_async_copy(image, image_in, in_sems.at[1])
     fetch_k.start()
     fetch_v.start()
+
+    def near(steps):
+        offsets = sorted({(x % GX, y % GY) for x in steps for y in steps} - {(0, 0)}, key=nearness)
+        return [(lax.rem(gx + x, GX), lax.rem(gy + y, GY)) for x, y in offsets]
+
+    def tell(n):
+        for peer in near((0, 2 << n, -2 << n)):
+            pl.semaphore_signal(known_sems.at[n], inc=1, device_id=peer, device_id_type=MESH)
+
+    def hear(n):
+        pl.semaphore_wait(known_sems.at[n], len(near((0, 2 << n, -2 << n))))
+
+    greeted = near(range(-2, 3))
+    for peer in greeted:
+        pl.semaphore_signal(barrier, inc=1, device_id=peer, device_id_type=MESH)
 
     lane0 = iota((16, 128), 1)
     odd_row = iota((16, 128), 0) & 1
@@ -162,26 +177,15 @@
         right = jnp.take_along_axis(values[:, 128:], second, axis=1)
         return jnp.where(low0, left, right), roll(jnp.where(low0, right, left), 64)
 
-    def join(red, black, par):
-        parity = odd_row ^ par
-        turned = roll(black, 64)
-        left, right = jnp.where(low0, red, turned), jnp.where(low0, turned, red)
-        same = (lane0 & 1) == parity
-        half = lane0 >> 1
-        first = half + jnp.where(same, 0, 64)
-        second = half + jnp.where(same, 64, 0)
-        return jnp.take_along_axis(left, first, axis=1), jnp.take_along_axis(right, second, axis=1)
     nothing = jnp.zeros((2, 4, 4, 8, 128), F32)
     kg[:, :, :, 0:8], kg[:, :, :, 40:48] = nothing, nothing
     nothing = jnp.zeros((2, 20, 8, 128), F32)
     v2[:, :, 0:8], v2[:, :, 40:48] = nothing, nothing
     nothing = jnp.zeros((2, 2, 48, 128), F32)
     v2[:, 0:2], v2[:, 18:20] = nothing, nothing
+    nothing = jnp.zeros((2, 4, 8, 128), F32)
     for ref in (k3, v3):
-        nothing = jnp.zeros((2, 10, 8, 128), F32)
         ref[:, :, 0:8], ref[:, :, 24:32] = nothing, nothing
-        nothing = jnp.zeros((2, 1, 32, 128), F32)
-        ref[:, 0:1], ref[:, 9:10] = nothing, nothing
 
     def zero(ref, *at):
         at = (slice(None),) * (len(ref.shape) - 3) + at
@@ -205,21 +209,24 @@
             for ref in (k1, s1x, vk1):
                 zero(ref, slice(None), cols1)
 
-    fetch_k.wait()
     for i in range(16):
+        if i == 0:
+            fetch_k.wait()
         kx[0, i + 5, 8:24], kx[1, i + 5, 8:24] = split(conduct_in[i], i & 1)
-    pl.semaphore_wait(barrier, len(ring(1)))
+
+    pl.semaphore_wait(barrier, len(greeted))
     cone = [(0, 2, 4), (2, 4, 2)]
-    send_k = halo_copies(kx, (5, 8), kx, (5, 8), (16, 16), (5, 5), halo_sems.at[0], position, cone)
-    send_v = halo_copies(vs, (0, 0), vx, (5, 8), (16, 16), (5, 5), halo_sems.at[1], position, cone)
+    send_k = halo_copies(kx, (5, 8), kx, (5, 8), (16, 16), (5, 5), (sent.at[0], arrived.at[0]), position, cone)
+    send_v = halo_copies(vs, (0, 0), vx, (5, 8), (16, 16), (5, 5), (sent.at[0], arrived.at[1]), position, cone)
+    tell(0)
     halo_start(send_k)
-    tell(0)
     fetch_v.wait()
     for i in range(16):
         red, black = split(image_in[i], i & 1)
         vx[0, i + 5, 8:24], vx[1, i + 5, 8:24] = red, black
         vs[0, i], vs[1, i] = red, black
     halo_start(send_v)
+
     def block_mean():
         return [0.125 * (t0[i, pl.ds(0, 8, stride=2)] + t0[i, pl.ds(1, 8, stride=2)]) for i in range(8)]
 
@@ -245,23 +252,22 @@
                 own2[kind, colour, a] = cells[colour]
                 whole[colour, chip_x, 2 * core + a, pl.ds(8 + 2 * gy, 2)] = cells[colour]
 
-    def remote(src, dst, sems, device):
+    def remote(src, dst, which, device):
         return pltpu.make_async_remote_copy(
-            src_ref=src, dst_ref=dst, send_sem=sems.at[0], recv_sem=sems.at[1], device_id=device, device_id_type=MESH
+            src_ref=src, dst_ref=dst, send_sem=sent.at[which // 9], recv_sem=arrived.at[which], device_id=device, device_id_type=MESH
         )
 
     cores_rows = pl.ds(2 * core, 2)
     own_place = (slice(None), chip_x, cores_rows, pl.ds(8 + 2 * gy, 2))
 
     spread_s = [
-        remote(own2.at[1], sg.at[own_place], gather_sems.at[x], chip) for chip, (x, _, _) in zip(chips, CHIPS)
+        remote(own2.at[1], sg.at[own_place], 9 + x, chip) for chip, (x, _, _) in zip(chips, CHIPS)
     ]
     planes = [sg.at[:, lax.rem(chip_x + 4 - x, 4), cores_rows, 8:40] for x in range(4)]
-    share_s = [remote(plane, plane, gather_sems.at[4 + x], sibling) for x, plane in enumerate(planes)]
-
-    def landed(x, which):
-        some = dummy.at[0:15] if x == 0 else dummy
-        pltpu.make_async_copy(some, some, gather_sems.at[x, which]).wait()
+    share_s = [remote(plane, plane, 13, sibling) for plane in planes]
+
+    def arrive(copies, which):
+        wait_rows(rows_of(copies), arrived.at[which], dummy)
 
     def chip_at(x, y, z):
         return (
@@ -272,11 +278,13 @@
     sheet = kg.at[:, :, cores_rows, pl.ds(8 + 8 * chip_z, 8)]
     half = kg.at[:, :, cores_rows, 8:40]
     tree_xy = [
-        remote(own2.at[0], kg.at[own_place], tree_sems.at[n], chip_at(x, y, 0))
-        for n, (x, y) in enumerate((x, y) for x in range(4) for y in range(4) if x or y)
+        remote(own2.at[0], kg.at[own_place], 6, chip_at(x, y, 0))
+        for x in range(4)
+        for y in range(4)
+        if x or y
     ]
-    tree_z = [remote(sheet, sheet, tree_sems.at[n + 14], chip_at(0, 0, n)) for n in (2, 1, 3)]
-    tree_core = [remote(half, half, tree_sems.at[18], sibling)]
+    tree_z = [remote(sheet, sheet, 7, chip_at(0, 0, n)) for n in (2, 1, 3)]
+    tree_core = [remote(half, half, 8, sibling)]
 
     for i in range(8):
         e = 2 * i + 5
@@ -285,7 +293,7 @@
     for a in range(4):
         k1[0, a + 4, 16:24], k1[1, a + 4, 16:24] = merge(rows[2 * a], rows[2 * a + 1], odd_8)
     level_2_share(0, [rows[2 * a] + rows[2 * a + 1] for a in range(4)], kg)
-    send_k1 = halo_copies(k1, (4, 16), k1, (4, 16), (4, 8), (3, 6), halo_sems.at[2], position)
+    send_k1 = halo_copies(k1, (4, 16), k1, (4, 16), (4, 8), (3, 6), (sent.at[0], arrived.at[2]), position)
     halo_start(send_k1)
 
     shape = (2, 24, 128)
@@ -300,9 +308,14 @@
         jnp.where(even_row, jnp.where(lanes == 127, 0.0, 0.5), jnp.where(lanes == 0, 0.0, 0.5)).astype(F32),
     ]
 
-    def beside(values, colour, rows_even):
-        below, above = roll(values, 1), roll(values, -1)
-        return jnp.where(rows_even, below, above) if colour == 0 else jnp.where(rows_even, above, below)
+    def beside(values, colour, even):
+        step = 1 if colour == 0 else -1
+        first = roll(jnp.where(even, values[0], values[1]), step)
+        second = roll(jnp.where(even, values[1], values[0]), -step)
+        return jnp.stack([jnp.where(even, first, second), jnp.where(even, second, first)])
+
+    even_24 = (iota((24, 128), 0) & 1) == 0
+    even_16 = (iota((16, 128), 0) & 1) == 0
 
     row_index = iota((2, 1, 1), 0)
 
@@ -318,7 +331,7 @@
                 (here + kx[1 - colour, e:e + 2, 3:27]) * wy_low,
                 (here + kx[1 - colour, e:e + 2, 5:29]) * wy_high,
                 (here + other) * 0.5,
-                (here + beside(other, colour, even_row)) * wz[colour],
+                (here + beside(other, colour, even_24)) * wz[colour],
             ]
             total = ((parts[0] + parts[1]) + (parts[2] + parts[3])) + ((parts[4] + parts[5]) + 1.0)
             inverse = 1.0 / total
@@ -340,22 +353,19 @@
         acc3 = c0[colour, 5, f:f + 2, here] * beside(other, colour, rows_even)
         return (acc0 + acc1) + (acc2 + acc3)
 
-    own_even = ((iota((2, 16, 128), 0) + iota((2, 16, 128), 1)) & 1) == 0
-
     def half_sweep_0(colour, start, stop, lo=-4, hi=20):
-        rows_even = even_row if hi - lo == 24 else own_even
+        rows_even = even_24 if hi - lo == 24 else even_16
         for i in range(start, stop, 2):
             vx[colour, i + 5:i + 7, lo + 8:hi + 8] = update_0(colour, i, lo, hi, rows_even)
+
+    halo_wait([send_k], position, arrived.at[0], dummy)
     hear(0)
     tell(1)
-    halo_wait(send_k)
     couplings_0(0, -4, 20)
     couplings_0(1, -4, 20)
-    hear(1)
-    tell(2)
     for copy in tree_xy:
         copy.start()
-    halo_wait(send_v)
+    halo_wait([send_v], position, arrived.at[1], dummy)
     for colour in (0, 1):
         for i in range(-4, 20, 2):
             s0[colour, i + 4:i + 6] = s0[colour, i + 4:i + 6] * vx[colour, i + 5:i + 7, 4:28]
@@ -364,10 +374,11 @@
     half_sweep_0(1, -4, 20)
     half_sweep_0(0, -2, 18)
     half_sweep_0(1, -2, 18)
+
     def residual_0(i):
         total = None
         for colour in (0, 1):
-            left = update_0(colour, i, 0, 16, own_even) - vx[colour, i + 5:i + 7, 8:24]
+            left = update_0(colour, i, 0, 16, even_16) - vx[colour, i + 5:i + 7, 8:24]
             left = d0[colour, i + 4:i + 6, 4:20] * left
             total = left if total is None else total + left
         return total
@@ -378,11 +389,11 @@
     rows = block_mean()
     for a in range(4):
         s1x[0, a + 4, 16:24], s1x[1, a + 4, 16:24] = merge(rows[2 * a], rows[2 * a + 1], odd_8)
-    send_s1 = halo_copies(s1x, (4, 16), s1x, (4, 16), (4, 8), (3, 5), halo_sems.at[3], position)
+    send_s1 = halo_copies(s1x, (4, 16), s1x, (4, 16), (4, 8), (3, 5), (sent.at[0], arrived.at[3]), position)
     halo_start(send_s1)
 
     vk[5:21, 8:24] = vx[1, 5:21, 8:24]
-    send_vk = halo_copies(vk, (5, 8), vk, (5, 8), (16, 16), (4, 4), halo_sems.at[4], position)
+    send_vk = halo_copies(vk, (5, 8), vk, (5, 8), (16, 16), (4, 4), (sent.at[0], arrived.at[4]), position)
     halo_start(send_vk)
 
     shape = (24, 128)
@@ -400,7 +411,8 @@
         return odd == 0, odd == 1
 
     first_24, first_16, first_8 = first_of_pair(24, 0), first_of_pair(16, 0), first_of_pair(8, 0)
-    halo_wait(send_k1)
+
+    halo_wait([send_k1], position, arrived.at[2], dummy)
     for colour in (0, 1):
         for a in range(-3, 7):
             e, f = a + 4, a + 3
@@ -431,13 +443,13 @@
     def half_sweep_1(colour, start, stop, lo, hi):
         for a in range(start, stop):
             v1[colour, a + 4, lo + 16:hi + 16] = update_1(colour, a, lo, hi)
-    hear(2)
-    for copy in tree_xy:
-        copy.wait_recv()
+
+    hear(1)
+    arrive(tree_xy, 6)
     for copy in tree_z:
         copy.start()
 
-    halo_wait(send_s1)
+    halo_wait([send_s1], position, arrived.at[3], dummy)
     for colour in (0, 1):
         for a in range(-3, 7):
             s1[colour, a + 3] = i1[colour, a + 3] * s1x[colour, a + 4, 10:34]
@@ -453,14 +465,13 @@
     level_2_share(1, pairs, sg)
     for copy in spread_s:
         copy.start()
-    for copy in tree_z:
-        copy.wait_recv()
+    arrive(tree_z, 7)
     tree_core[0].start()
     vk1[4:8, 16:24] = v1[1, 4:8, 16:24]
-    send_vk1 = halo_copies(vk1, (4, 16), vk1, (4, 16), (4, 8), (3, 6), halo_sems.at[5], position)
+    send_vk1 = halo_copies(vk1, (4, 16), vk1, (4, 16), (4, 8), (3, 6), (sent.at[0], arrived.at[5]), position)
     halo_start(send_vk1)
 
-    tree_core[0].wait_recv()
+    arrive(tree_core, 8)
     def two_columns(size):
         return iota((size, 128), 1) < 64, (iota((size, 128), 0) & 1) == 1
 
@@ -504,6 +515,7 @@
             i2[colour, a] = inverse
             for n in range(6):
                 c2[colour, n, a] = parts[n]
+
     lane3 = iota((16, 128), 1)
     even_place = (lane3 & 1) == 0
     place3 = (lane3 & 63) >> 1
@@ -512,13 +524,16 @@
     odd3 = (((lane3 >> 6) + place3) & 1) == 1
     first3 = (jnp.logical_not(odd3), odd3)
 
-    def level_3_share(p, pairs):
+    lower = even_place
+
+    def level_3_share(p):
         rows = []
-        for n in range(2):
-            t2[2 * p + n] = pairs[n]
-        for n in range(2):
-            row = t2[2 * p + n, pl.ds(0, 16, stride=2)] + t2[2 * p + n, pl.ds(1, 16, stride=2)]
-            rows.append(0.125 * (row + jnp.where(even_place, roll(row, -1), roll(row, 1))))
+        for n in (2 * p, 2 * p + 1):
+            both = []
+            for a in (n, n + 8):
+                row = t2[a, pl.ds(0, 16, stride=2)] + t2[a, pl.ds(1, 16, stride=2)]
+                both.append(row + jnp.where(even_place, roll(row, -1), roll(row, 1)))
+            rows.append(0.125 * jnp.where(lower, both[0], both[1]))
         return merge(rows[0], rows[1], odd3)
 
     w3 = 0.5 / 64.0
@@ -529,34 +544,40 @@
     at3 = slice(8, 24)
 
     def around_3(ref, colour, p, first):
-        here = ref[colour, p + 1, at3]
-        cross = jnp.where(first, ref[colour, p, at3], ref[colour, p + 2, at3])
-        low = roll(jnp.where(low3, here, ref[colour, p + 1, 7:23]), 64)
-        high = roll(jnp.where(low3, ref[colour, p + 1, 9:25], here), 64)
-        return here, cross, low, high
-
-    for p in range(8):
-        pairs = [kg_rows(0, a, at) + kg_rows(1, a, at) for a in (2 * p, 2 * p + 1)]
-        k3[0, p + 1, at3], k3[1, p + 1, at3] = level_3_share(p, pairs)
+        here = ref[colour, p, at3]
+        before = ref[colour, p - 1, at3] if p else roll(ref[colour, 3, at3], 1)
+        after = ref[colour, p + 1, at3] if p < 3 else roll(ref[colour, 0, at3], -1)
+        low = roll(jnp.where(low3, here, ref[colour, p, 7:23]), 64)
+        high = roll(jnp.where(low3, ref[colour, p, 9:25], here), 64)
+        return here, jnp.where(first, before, after), low, high
+
+    for a in range(16):
+        t2[a] = kg_rows(0, a, at) + kg_rows(1, a, at)
+    for p in range(4):
+        k3[0, p, at3], k3[1, p, at3] = level_3_share(p)
     for colour in (0, 1):
-        for p in range(8):
+        for p in range(4):
             here, cross, low, high = around_3(k3, 1 - colour, p, first3[colour])
             w_cross = w3
             if p == 0:
-                w_cross = jnp.where(first3[colour], 0.0, w3).astype(F32)
-            if p == 7:
-                w_cross = jnp.where(first3[colour], w3, 0.0).astype(F32)
+                w_cross = jnp.where(first3[colour] & lower, 0.0, w3).astype(F32)
+            if p == 3:
+                w_cross = jnp.where(first3[colour] | lower, w3, 0.0).astype(F32)
             parts, _, inverse = couple(
-                k3[colour, p + 1, at3], here, cross, low, high, here, (w3, w_cross, wy_low, wy_high, wz_low, wz_high), 2
+                k3[colour, p, at3], here, cross, low, high, here, (w3, w_cross, wy_low, wy_high, wz_low, wz_high), 2
             )
             i3[colour, p] = inverse
             for n in range(6):
                 c3[colour, n, p] = parts[n]
+
+    halo_wait(
+        [send_k, send_v, send_k1, send_s1, send_vk, send_vk1], position, sent.at[0], dummy,
+        rows_of(tree_xy + tree_z + tree_core),
+    )
     for x in (0, 1, 3, 2):
-        landed(x, 1)
+        arrive([copy for copy, chip in zip(spread_s, CHIPS) if chip[0] == x], 9 + x)
         share_s[x].start()
-    for copy in share_s:
-        copy.wait_recv()
+    arrive(share_s, 13)
 
     for colour in (0, 1):
         for a in range(16):
@@ -583,34 +604,36 @@
     half_sweep_2(1)
     half_sweep_2(0)
     half_sweep_2(1)
-    for p in range(8):
-        pairs = []
-        for a in (2 * p, 2 * p + 1):
-            left = [d2[n, a] * (update_2(n, a, *whole_2) - v2[n, a + 2, at]) for n in (0, 1)]
-            pairs.append(left[0] + left[1])
-        sources = level_3_share(p, pairs)
+    for a in range(16):
+        left = [d2[n, a] * (update_2(n, a, *whole_2) - v2[n, a + 2, at]) for n in (0, 1)]
+        t2[a] = left[0] + left[1]
+    for p in range(4):
+        sources = level_3_share(p)
         for colour in (0, 1):
             s3[colour, p] = i3[colour, p] * sources[colour]
 
     def half_sweep_3(colour):
-        for p in range(8):
+        for p in range(4):
             here, cross, low, high = around_3(v3, 1 - colour, p, first3[colour])
-            v3[colour, p + 1, at3] = relax(
+            v3[colour, p, at3] = relax(
                 s3[colour, p], [c3[colour, n, p] for n in range(6)], here, cross, low, high, 2
             )
 
-    for p in range(8):
-        v3[0, p + 1, at3] = s3[0, p]
+    for p in range(4):
+        v3[0, p, at3] = s3[0, p]
     half_sweep_3(1)
     for _ in range(COARSE_SWEEPS - 1):
         half_sweep_3(0)
         half_sweep_3(1)
 
-    for p in range(8):
-        red, black = v3[0, p + 1, at3], v3[1, p + 1, at3]
-        for n, row in enumerate((jnp.where(odd3, black, red), jnp.where(odd3, red, black))):
-            p2[2 * p + n, pl.ds(0, 16, stride=2)] = row
-            p2[2 * p + n, pl.ds(1, 16, stride=2)] = row
+    for p in range(4):
+        cells = [v3[colour, p, at3] for colour in (0, 1)]
+        firsts = [jnp.where(lower, c, roll(c, 1)) for c in cells]
+        seconds = [jnp.where(lower, roll(c, -1), c) for c in cells]
+        for pair, (red, black) in ((p, firsts), (p + 4, seconds)):
+            for n, row in enumerate((jnp.where(odd3, black, red), jnp.where(odd3, red, black))):
+                p2[2 * pair + n, pl.ds(0, 16, stride=2)] = row
+                p2[2 * pair + n, pl.ds(1, 16, stride=2)] = row
 
     def within(value, top, span):
         value = value * ((value + span) // span)
@@ -640,7 +663,7 @@
                 column = q1[d, n, pl.ds(m, 4, stride=2)]
                 p1[d, pl.ds(4 * n + 2 * m, 4, stride=8)] = column
                 p1[d, pl.ds(4 * n + 2 * m + 1, 4, stride=8)] = column
-    halo_wait(send_vk1)
+    halo_wait([send_vk1], position, arrived.at[5], dummy)
     for a in range(-3, 7):
         v1[1, a + 4, 10:30] = vk1[a + 4, 10:30] + p1[a + 3, 2:22]
     half_sweep_1(0, -3, 7, -6, 18)
@@ -654,21 +677,37 @@
         row = jnp.where(odd_12 == i % 2, v1[0, a + 4, 14:26], v1[1, a + 4, 14:26])
         p0[i + 2, pl.ds(0, 12, stride=2)] = row
         p0[i + 2, pl.ds(1, 12, stride=2)] = row
-    halo_wait(send_vk)
+    halo_wait([send_vk], position, arrived.at[4], dummy)
     for i in range(-4, 20):
         vx[1, i + 5, 4:28] = vk[i + 5, 4:28] + p0[i // 2 + 2]
     half_sweep_0(0, -4, 20)
     half_sweep_0(1, -2, 18)
     half_sweep_0(0, -2, 18)
-    half_sweep_0(1, 0, 16, 0, 16)
+    for i in range(0, 16, 2):
+        out[0, i:i + 2] = vx[0, i + 5:i + 7, 8:24]
+        out[1, i:i + 2] = update_0(1, i, 0, 16, even_16)
+
+    wait_rows(rows_of(spread_s + share_s), sent.at[1], dummy)
+
+
+def join(cells, out, rows, sems):
+    lane = iota((16, 128), 1)
+    odd_row = iota((16, 128), 0) & 1
+    low = lane < 64
+    half = lane >> 1
+    copies = []
     for i in range(16):
-        out[i, :, :128], out[i, :, 128:] = join(vx[0, i + 5, 8:24], vx[1, i + 5, 8:24], i & 1)
-    for copies in (send_k, send_v, send_k1, send_s1, send_vk, send_vk1):
-        halo_sent(copies)
-    for copy in tree_xy + tree_z + tree_core + share_s:
-        copy.wait_send()
-    for x in range(4):
-        landed(x, 0)
+        red, turned = cells[0, i], roll(cells[1, i], 64)
+        left, right = jnp.where(low, red, turned), jnp.where(low, turned, red)
+        same = (lane & 1) == (odd_row ^ (i & 1))
+        rows[i, :, :128] = jnp.take_along_axis(left, half + jnp.where(same, 0, 64), axis=1)
+        rows[i, :, 128:] = jnp.take_along_axis(right, half + jnp.where(same, 64, 0), axis=1)
+        if i % 4 == 3:
+            part = pl.ds(i - 3, 4)
+            copies.append(pltpu.make_async_copy(rows.at[part], out.at[part], sems.at[i // 4]))
+            copies[-1].start()
+    for copy in copies:
+        copy.wait()
 
 
 def v_cycle(image, conduct):
@@ -676,9 +715,9 @@
         return pltpu.VMEM(shape, F32)
 
     frame0, frame1, gathered = (26, 32, 128), (12, 40, 128), (2, 4, 4, 48, 128)
-    return pl.pallas_call(
+    cells = pl.pallas_call(
         kernel,
-        out_shape=jax.ShapeDtypeStruct((16, 16, 256), F32),
+        out_shape=jax.ShapeDtypeStruct((2, 16, 16, 128), F32),
         in_specs=[pl.BlockSpec(memory_space=pltpu.HBM)] * 2,
         out_specs=pl.BlockSpec(memory_space=pltpu.VMEM),
         scratch_shapes=[
@@ -690,16 +729,25 @@
             vmem(10, 2, 8, 128), vmem(2, 2, 2, 2, 128), vmem(*gathered), vmem(*gathered), vmem(2, 20, 48, 128),
             vmem(2, 6, 16, 32, 128), vmem(2, 16, 32, 128), vmem(2, 16, 32, 128), vmem(2, 16, 32, 128), vmem(16, 32, 128),
             vmem(16, 32, 128),
-            vmem(2, 10, 32, 128), vmem(2, 10, 32, 128), vmem(2, 6, 8, 16, 128), vmem(2, 8, 16, 128),
-            vmem(2, 8, 16, 128), vmem(16, 8, 128),
-            pltpu.SemaphoreType.DMA((6, 2, 12)), pltpu.SemaphoreType.DMA((8, 2)), pltpu.SemaphoreType.DMA((19, 2)),
-            pltpu.SemaphoreType.DMA((2,)), pltpu.SemaphoreType.REGULAR((3,)),
+            vmem(2, 4, 32, 128), vmem(2, 4, 32, 128), vmem(2, 6, 4, 16, 128), vmem(2, 4, 16, 128),
+            vmem(2, 4, 16, 128), vmem(4096, 128),
+            pltpu.SemaphoreType.DMA((2,)), pltpu.SemaphoreType.DMA((14,)), pltpu.SemaphoreType.DMA((2,)),
+            pltpu.SemaphoreType.REGULAR((2,)),
         ],
         compiler_params=pltpu.CompilerParams(
             collective_id=0, has_side_effects=True, vmem_limit_bytes=48 * 2**20
         ),
         name="v_cycle",
-    )(image, conduct)
+    )(*(pltpu.with_memory_space_constraint(array, pltpu.HBM) for array in (image, conduct)))
+    return pl.pallas_call(
+        join,
+        out_shape=jax.ShapeDtypeStruct((16, 16, 256), F32),
+        in_specs=[pl.BlockSpec(memory_space=pltpu.VMEM)],
+        out_specs=pl.BlockSpec(memory_space=pltpu.HBM),
+        scratch_shapes=[vmem(16, 16, 256), pltpu.SemaphoreType.DMA((4,))],
+        compiler_params=pltpu.CompilerParams(vmem_limit_bytes=8 * 2**20),
+        name="join",
+    )(cells)
 
 
 def solution(mesh):

time: 39.9 us -> 35.8 us (0.90)
  local copies, waits for them, and re-layouts: 2.6 us -> 0 us
  Pallas kernels: 37 us -> 35.6 us
    unnamed x5 -> x0, local copies, waits for them, and re-layouts: 2.6 us -> none
    pallas_call x1 -> x2, Pallas kernels: 37 us -> 35.6 us  [the longest x1 34.6 us: v_cycle(): pl.pallas_call(kernel, out_shape=jax.ShapeDtypeStruct((2, 16, 16, 128), F...]
where the time goes in v5:
time: 35.8 us; the launch traced here: 35.6 us
  Pallas kernels  35.6 us (99%)
    pallas_call x1, Pallas kernels, v_cycle(): pl.pallas_call(kernel, out_shape=jax.ShapeDtypeStruct((2, 16, 16, 128), F...  34.6 us
    pallas_call x1, Pallas kernels, v_cycle(): pl.pallas_call(join, out_shape=jax.ShapeDtypeStruct((16, 16, 256), F32),...  1.07 us

profile of v5, /device:TPU:1, one launch (start us, length us, event | category | flops | bytes accessed | tf_op | source)
XLA Modules:
  0.0 35.6 jit_solution(117705822876238589)
XLA Ops:
  0.0 34.6 %v_cycle.1.cells = f32[2,16,16,128]{3,2,1,0:T(8,128)S(1)} custom-call(f32[16,16,256]{2,1,0:T(8,128)} %image.1, f32[16,16,256]{2,1,0:T(8,128)} %conduct.1), custom_call_target="tpu_custom_call" | custom-call | tf_op jit(solution)/shard_map/v_cycle/pallas_call | solution.py:718
  34.6 1.1 %join.1 = f32[16,16,256]{2,1,0:T(8,128)} custom-call(f32[2,16,16,128]{3,2,1,0:T(8,128)S(1)} %v_cycle.1.cells), custom_call_target="tpu_custom_call" | custom-call | tf_op jit(solution)/shard_map/join/pallas_call | solution.py:742

commit v6 on v5

--- a/solution.py
+++ b/solution.py
@@ -30,9 +30,9 @@
     return pltpu.roll(values, shift % 128, values.ndim - 1)
 
 
-def halo_copies(src, src_origin, dst, origin, extent, widths, sems, position, corners=None):
+def halo_copies(src, src_origin, dst, origin, extent, widths, sems, position, corners=None, colour=None):
     gx, gy = position
-    lead = (slice(None),) * (len(dst.shape) - 3)
+    lead = (slice(None),) * (len(dst.shape) - 3) if colour is None else (colour,)
 
     def piece(step, size, here, there, start, stop):
         if step == 0:
@@ -160,7 +160,7 @@
     def hear(n):
         pl.semaphore_wait(known_sems.at[n], len(near((0, 2 << n, -2 << n))))
 
-    greeted = near(range(-2, 3))
+    greeted = near(range(-2, 3)) + [(lax.rem(gx + 4, GX), gy)]
     for peer in greeted:
         pl.semaphore_signal(barrier, inc=1, device_id=peer, device_id_type=MESH)
 
@@ -215,9 +215,17 @@
         kx[0, i + 5, 8:24], kx[1, i + 5, 8:24] = split(conduct_in[i], i & 1)
 
     pl.semaphore_wait(barrier, len(greeted))
-    cone = [(0, 2, 4), (2, 4, 2)]
-    send_k = halo_copies(kx, (5, 8), kx, (5, 8), (16, 16), (5, 5), (sent.at[0], arrived.at[0]), position, cone)
-    send_v = halo_copies(vs, (0, 0), vx, (5, 8), (16, 16), (5, 5), (sent.at[0], arrived.at[1]), position, cone)
+    def halos(src, src_origin, dst, origin, extent, which, *cones):
+        sems = (sent.at[0], arrived.at[which])
+        each = [
+            halo_copies(src, src_origin, dst, origin, extent, widths, sems, position, corners, colour)
+            for colour, widths, corners in cones
+        ]
+        return [(ways[0][0], sum((group for _, group in ways), [])) for ways in zip(*each)]
+
+    cones = (1, (5, 5), [(0, 2, 4), (2, 4, 2)]), (0, (4, 4), [(0, 3, 3)])
+    send_k = halos(kx, (5, 8), kx, (5, 8), (16, 16), 0, *cones)
+    send_v = halos(vs, (0, 0), vx, (5, 8), (16, 16), 1, *cones)
     tell(0)
     halo_start(send_k)
     fetch_v.wait()
@@ -254,7 +262,7 @@
 
     def remote(src, dst, which, device):
         return pltpu.make_async_remote_copy(
-            src_ref=src, dst_ref=dst, send_sem=sent.at[which // 9], recv_sem=arrived.at[which], device_id=device, device_id_type=MESH
+            src_ref=src, dst_ref=dst, send_sem=sent.at[int(9 <= which <= 13)], recv_sem=arrived.at[which], device_id=device, device_id_type=MESH
         )
 
     cores_rows = pl.ds(2 * core, 2)
@@ -275,15 +283,12 @@
             lax.rem(chip_z + z, 4) * 4 + lax.rem(chip_y + y, 4),
         )
 
+    row = kg.at[:, :, cores_rows, pl.ds(8 + 2 * gy, 2)]
     sheet = kg.at[:, :, cores_rows, pl.ds(8 + 8 * chip_z, 8)]
     half = kg.at[:, :, cores_rows, 8:40]
-    tree_xy = [
-        remote(own2.at[0], kg.at[own_place], 6, chip_at(x, y, 0))
-        for x in range(4)
-        for y in range(4)
-        if x or y
-    ]
-    tree_z = [remote(sheet, sheet, 7, chip_at(0, 0, n)) for n in (2, 1, 3)]
+    tree_x = [remote(own2.at[0], kg.at[own_place], 6, chip_at(n, 0, 0)) for n in (2, 1, 3)]
+    tree_y = [remote(row, row, 7, chip_at(0, n, 0)) for n in (2, 1, 3)]
+    tree_z = [remote(sheet, sheet, 14, chip_at(0, 0, n)) for n in (2, 1, 3)]
     tree_core = [remote(half, half, 8, sibling)]
 
     for i in range(8):
@@ -293,7 +298,7 @@
     for a in range(4):
         k1[0, a + 4, 16:24], k1[1, a + 4, 16:24] = merge(rows[2 * a], rows[2 * a + 1], odd_8)
     level_2_share(0, [rows[2 * a] + rows[2 * a + 1] for a in range(4)], kg)
-    send_k1 = halo_copies(k1, (4, 16), k1, (4, 16), (4, 8), (3, 6), (sent.at[0], arrived.at[2]), position)
+    send_k1 = halos(k1, (4, 16), k1, (4, 16), (4, 8), 2, (None, (3, 6), [(0, 1, 6), (1, 3, 4)]))
     halo_start(send_k1)
 
     shape = (2, 24, 128)
@@ -358,12 +363,15 @@
         for i in range(start, stop, 2):
             vx[colour, i + 5:i + 7, lo + 8:hi + 8] = update_0(colour, i, lo, hi, rows_even)
 
+    for copy in tree_x:
+        copy.start()
     halo_wait([send_k], position, arrived.at[0], dummy)
+    couplings_0(0, -4, 20)
+    couplings_0(1, -4, 20)
     hear(0)
     tell(1)
-    couplings_0(0, -4, 20)
-    couplings_0(1, -4, 20)
-    for copy in tree_xy:
+    arrive(tree_x, 6)
+    for copy in tree_y:
         copy.start()
     halo_wait([send_v], position, arrived.at[1], dummy)
     for colour in (0, 1):
@@ -389,11 +397,11 @@
     rows = block_mean()
     for a in range(4):
         s1x[0, a + 4, 16:24], s1x[1, a + 4, 16:24] = merge(rows[2 * a], rows[2 * a + 1], odd_8)
-    send_s1 = halo_copies(s1x, (4, 16), s1x, (4, 16), (4, 8), (3, 5), (sent.at[0], arrived.at[3]), position)
+    send_s1 = halos(s1x, (4, 16), s1x, (4, 16), (4, 8), 3, (None, (3, 5), [(0, 1, 5), (1, 3, 3)]))
     halo_start(send_s1)
 
     vk[5:21, 8:24] = vx[1, 5:21, 8:24]
-    send_vk = halo_copies(vk, (5, 8), vk, (5, 8), (16, 16), (4, 4), (sent.at[0], arrived.at[4]), position)
+    send_vk = halos(vk, (5, 8), vk, (5, 8), (16, 16), 4, (None, (4, 4), None))
     halo_start(send_vk)
 
     shape = (24, 128)
@@ -445,7 +453,7 @@
             v1[colour, a + 4, lo + 16:hi + 16] = update_1(colour, a, lo, hi)
 
     hear(1)
-    arrive(tree_xy, 6)
+    arrive(tree_y, 7)
     for copy in tree_z:
         copy.start()
 
@@ -465,10 +473,10 @@
     level_2_share(1, pairs, sg)
     for copy in spread_s:
         copy.start()
-    arrive(tree_z, 7)
+    arrive(tree_z, 14)
     tree_core[0].start()
     vk1[4:8, 16:24] = v1[1, 4:8, 16:24]
-    send_vk1 = halo_copies(vk1, (4, 16), vk1, (4, 16), (4, 8), (3, 6), (sent.at[0], arrived.at[5]), position)
+    send_vk1 = halos(vk1, (4, 16), vk1, (4, 16), (4, 8), 5, (None, (3, 6), None))
     halo_start(send_vk1)
 
     arrive(tree_core, 8)
@@ -572,7 +580,7 @@
 
     halo_wait(
         [send_k, send_v, send_k1, send_s1, send_vk, send_vk1], position, sent.at[0], dummy,
-        rows_of(tree_xy + tree_z + tree_core),
+        rows_of(tree_x + tree_y + tree_z + tree_core),
     )
     for x in (0, 1, 3, 2):
         arrive([copy for copy, chip in zip(spread_s, CHIPS) if chip[0] == x], 9 + x)
@@ -731,7 +739,7 @@
             vmem(16, 32, 128),
             vmem(2, 4, 32, 128), vmem(2, 4, 32, 128), vmem(2, 6, 4, 16, 128), vmem(2, 4, 16, 128),
             vmem(2, 4, 16, 128), vmem(4096, 128),
-            pltpu.SemaphoreType.DMA((2,)), pltpu.SemaphoreType.DMA((14,)), pltpu.SemaphoreType.DMA((2,)),
+            pltpu.SemaphoreType.DMA((2,)), pltpu.SemaphoreType.DMA((15,)), pltpu.SemaphoreType.DMA((2,)),
             pltpu.SemaphoreType.REGULAR((2,)),
         ],
         compiler_params=pltpu.CompilerParams(

time: 35.8 us -> 35 us (0.978)
  Pallas kernels: 35.6 us -> 34.9 us
    pallas_call x1, Pallas kernels: 34.6 us -> 33.8 us  [v_cycle(): pl.pallas_call(kernel, out_shape=jax.ShapeDtypeStruct((2, 16, 16, 128), F...]
where the time goes in v6:
time: 35 us; the launch traced here: 34.9 us
  Pallas kernels  34.9 us (100%)
    pallas_call x1, Pallas kernels, v_cycle(): pl.pallas_call(kernel, out_shape=jax.ShapeDtypeStruct((2, 16, 16, 128), F...  33.8 us
    pallas_call x1, Pallas kernels, v_cycle(): pl.pallas_call(join, out_shape=jax.ShapeDtypeStruct((16, 16, 256), F32),...  1.07 us

profile of v6, /device:TPU:1, one launch (start us, length us, event | category | flops | bytes accessed | tf_op | source)
XLA Modules:
  0.0 34.9 jit_solution(1816047905110084021)
XLA Ops:
  0.0 33.8 %v_cycle.1.cells = f32[2,16,16,128]{3,2,1,0:T(8,128)S(1)} custom-call(f32[16,16,256]{2,1,0:T(8,128)} %image.1, f32[16,16,256]{2,1,0:T(8,128)} %conduct.1), custom_call_target="tpu_custom_call" | custom-call | tf_op jit(solution)/shard_map/v_cycle/pallas_call | solution.py:726
  33.8 1.1 %join.1 = f32[16,16,256]{2,1,0:T(8,128)} custom-call(f32[2,16,16,128]{3,2,1,0:T(8,128)S(1)} %v_cycle.1.cells), custom_call_target="tpu_custom_call" | custom-call | tf_op jit(solution)/shard_map/join/pallas_call | solution.py:750

commit v7 on v6

--- a/solution.py
+++ b/solution.py
@@ -298,7 +298,7 @@
     for a in range(4):
         k1[0, a + 4, 16:24], k1[1, a + 4, 16:24] = merge(rows[2 * a], rows[2 * a + 1], odd_8)
     level_2_share(0, [rows[2 * a] + rows[2 * a + 1] for a in range(4)], kg)
-    send_k1 = halos(k1, (4, 16), k1, (4, 16), (4, 8), 2, (None, (3, 6), [(0, 1, 6), (1, 3, 4)]))
+    send_k1 = halos(k1, (4, 16), k1, (4, 16), (4, 8), 2, (0, (3, 5), [(0, 1, 5), (1, 3, 3)]), (1, (3, 6), [(0, 1, 6), (1, 3, 4)]))
     halo_start(send_k1)
 
     shape = (2, 24, 128)
@@ -400,9 +400,6 @@
     send_s1 = halos(s1x, (4, 16), s1x, (4, 16), (4, 8), 3, (None, (3, 5), [(0, 1, 5), (1, 3, 3)]))
     halo_start(send_s1)
 
-    vk[5:21, 8:24] = vx[1, 5:21, 8:24]
-    send_vk = halos(vk, (5, 8), vk, (5, 8), (16, 16), 4, (None, (4, 4), None))
-    halo_start(send_vk)
 
     shape = (24, 128)
     col, lanes = iota(shape, 0) - 6, iota(shape, 1)
@@ -457,6 +454,9 @@
     for copy in tree_z:
         copy.start()
 
+    vk[5:21, 8:24] = vx[1, 5:21, 8:24]
+    send_vk = halos(vk, (5, 8), vk, (5, 8), (16, 16), 4, (None, (4, 4), None))
+    halo_start(send_vk)
     halo_wait([send_s1], position, arrived.at[3], dummy)
     for colour in (0, 1):
         for a in range(-3, 7):
@@ -578,10 +578,6 @@
             for n in range(6):
                 c3[colour, n, p] = parts[n]
 
-    halo_wait(
-        [send_k, send_v, send_k1, send_s1, send_vk, send_vk1], position, sent.at[0], dummy,
-        rows_of(tree_x + tree_y + tree_z + tree_core),
-    )
     for x in (0, 1, 3, 2):
         arrive([copy for copy, chip in zip(spread_s, CHIPS) if chip[0] == x], 9 + x)
         share_s[x].start()
@@ -695,6 +691,10 @@
         out[0, i:i + 2] = vx[0, i + 5:i + 7, 8:24]
         out[1, i:i + 2] = update_0(1, i, 0, 16, even_16)
 
+    halo_wait(
+        [send_k, send_v, send_k1, send_s1, send_vk, send_vk1], position, sent.at[0], dummy,
+        rows_of(tree_x + tree_y + tree_z + tree_core),
+    )
     wait_rows(rows_of(spread_s + share_s), sent.at[1], dummy)
 
 

time: 35 us -> 34.9 us (level)
  no operation moved by 1% of the time
where the time goes in v7:
time: 34.9 us; the launch traced here: 34.7 us
  Pallas kernels  34.7 us (99%)
    pallas_call x1, Pallas kernels, v_cycle(): pl.pallas_call(kernel, out_shape=jax.ShapeDtypeStruct((2, 16, 16, 128), F...  33.7 us
    pallas_call x1, Pallas kernels, v_cycle(): pl.pallas_call(join, out_shape=jax.ShapeDtypeStruct((16, 16, 256), F32),...  1.07 us

profile of v7, /device:TPU:1, one launch (start us, length us, event | category | flops | bytes accessed | tf_op | source)
XLA Modules:
  0.0 34.7 jit_solution(16152102362714560388)
XLA Ops:
  0.0 33.7 %v_cycle.1.cells = f32[2,16,16,128]{3,2,1,0:T(8,128)S(1)} custom-call(f32[16,16,256]{2,1,0:T(8,128)} %image.1, f32[16,16,256]{2,1,0:T(8,128)} %conduct.1), custom_call_target="tpu_custom_call" | custom-call | tf_op jit(solution)/shard_map/v_cycle/pallas_call | solution.py:726
  33.7 1.1 %join.1 = f32[16,16,256]{2,1,0:T(8,128)} custom-call(f32[2,16,16,128]{3,2,1,0:T(8,128)S(1)} %v_cycle.1.cells), custom_call_target="tpu_custom_call" | custom-call | tf_op jit(solution)/shard_map/join/pallas_call | solution.py:750

commit v8 on v7

--- a/solution.py
+++ b/solution.py
@@ -223,7 +223,7 @@
         ]
         return [(ways[0][0], sum((group for _, group in ways), [])) for ways in zip(*each)]
 
-    cones = (1, (5, 5), [(0, 2, 4), (2, 4, 2)]), (0, (4, 4), [(0, 3, 3)])
+    cones = (1, (5, 5), [(0, 2, 4), (2, 4, 2)]), (0, (4, 4), [(0, 1, 3), (1, 3, 2)])
     send_k = halos(kx, (5, 8), kx, (5, 8), (16, 16), 0, *cones)
     send_v = halos(vs, (0, 0), vx, (5, 8), (16, 16), 1, *cones)
     tell(0)
@@ -397,7 +397,7 @@
     rows = block_mean()
     for a in range(4):
         s1x[0, a + 4, 16:24], s1x[1, a + 4, 16:24] = merge(rows[2 * a], rows[2 * a + 1], odd_8)
-    send_s1 = halos(s1x, (4, 16), s1x, (4, 16), (4, 8), 3, (None, (3, 5), [(0, 1, 5), (1, 3, 3)]))
+    send_s1 = halos(s1x, (4, 16), s1x, (4, 16), (4, 8), 3, (0, (3, 5), None), (1, (2, 4), None))
     halo_start(send_s1)
 
 

time: 34.9 us -> 34.8 us (level)
  no operation moved by 1% of the time
where the time goes in v8:
time: 34.8 us; the launch traced here: 34.7 us
  Pallas kernels  34.7 us (100%)
    pallas_call x1, Pallas kernels, v_cycle(): pl.pallas_call(kernel, out_shape=jax.ShapeDtypeStruct((2, 16, 16, 128), F...  33.6 us
    pallas_call x1, Pallas kernels, v_cycle(): pl.pallas_call(join, out_shape=jax.ShapeDtypeStruct((16, 16, 256), F32),...  1.07 us

profile of v8, /device:TPU:1, one launch (start us, length us, event | category | flops | bytes accessed | tf_op | source)
XLA Modules:
  0.0 34.7 jit_solution(14681633540606822992)
XLA Ops:
  0.0 33.6 %v_cycle.1.cells = f32[2,16,16,128]{3,2,1,0:T(8,128)S(1)} custom-call(f32[16,16,256]{2,1,0:T(8,128)} %image.1, f32[16,16,256]{2,1,0:T(8,128)} %conduct.1), custom_call_target="tpu_custom_call" | custom-call | tf_op jit(solution)/shard_map/v_cycle/pallas_call | solution.py:726
  33.6 1.1 %join.1 = f32[16,16,256]{2,1,0:T(8,128)} custom-call(f32[2,16,16,128]{3,2,1,0:T(8,128)S(1)} %v_cycle.1.cells), custom_call_target="tpu_custom_call" | custom-call | tf_op jit(solution)/shard_map/join/pallas_call | solution.py:750
